TPU v7x, 32 devices: a whole 2x2x4 slice. The times are simulated.
32 devices in a mesh: pos: 4 (over x, core), filt: 4 (over z), layer: 2 (over y).
Axes of the slice: x: 2, y: 2, z: 4, core: 2. Of those that a mesh axis runs over, the one named last changes fastest.
Arguments:
- activations: float32 [128, 1024, 128], P('pos', ('layer', 'filt')), may hold values from -6 to 6
- filters: float32 [9, 1024, 1024], P(None, ('layer', 'pos'), 'filt'), may hold values from -0.0625 to 0.0625
Outputs:
- rectified: float32 [128, 1024, 128], P('pos', ('filt', 'layer'))
All inputs are finite; a program needn't handle non-finite values.
Results may differ from a plain program's by a relative error of at most 0.0001.
Values sent between devices are 32-bit elements; how exact they have to be, the bound alone decides.
No kernel may reach another device: no remote copies, remote signals or barrier semaphores. Data moves between devices by JAX's collectives and lax.ppermute only.
A program may use at most 128 MiB of HBM per device.

v0:
```python
import jax
import jax.numpy as jnp
from jax import lax
from jax.sharding import PartitionSpec as P


def extended(block, sides, width):
    for axis, dim in sides:
        count = lax.axis_size(axis)
        forward = [(i, i + 1) for i in range(count - 1)]
        backward = [(target, source) for source, target in forward]
        low = lax.ppermute(
            lax.slice_in_dim(block, block.shape[dim] - width, None, axis=dim), axis, forward
        )
        high = lax.ppermute(lax.slice_in_dim(block, 0, width, axis=dim), axis, backward)
        block = jnp.concatenate([low, block, high], axis=dim)
    return block


def convolve(padded, weights, summed):
    height = padded.shape[0] - 2
    across = padded.shape[2] - 2
    for tap_index in range(9):
        row_shift, col_shift = divmod(tap_index, 3)
        window = padded[row_shift : row_shift + height, :, col_shift : col_shift + across]
        summed = summed + jnp.einsum(
            "ric,io->roc", window, weights[tap_index], precision=lax.Precision.HIGHEST
        )
    return summed


def body(activations, filters):
    panel = lax.all_gather(activations, "filt", axis=1, tiled=True)
    rimmed = extended(panel, (("pos", 0),), 1)
    padded = jnp.pad(rimmed, ((0, 0), (0, 0), (1, 1)))
    height = activations.shape[0]
    across = activations.shape[2]
    empty = jnp.zeros((height, filters.shape[2], across), jnp.float32)
    gathered = lax.all_gather(filters, "pos", axis=1, tiled=True)
    summed = convolve(padded, gathered, empty)
    reduced = lax.psum_scatter(summed, "layer", scatter_dimension=1, tiled=True)
    return jnp.maximum(reduced, 0.0)


def solution(mesh):
    in_specs = (P("pos", ("layer", "filt"), None), P(None, ("layer", "pos"), "filt"))
    out_specs = P("pos", ("filt", "layer"), None)
    return jax.shard_map(body, mesh=mesh, in_specs=in_specs, out_specs=out_specs, check_vma=False)
```

profile of v0, /device:TPU:16, one launch (start us, length us, event | category | flops | bytes accessed | tf_op | source)
XLA Modules:
  0.0 350.5 jit_solution(5655809892816998642)
XLA Ops:
  6.5 2.9 copy.3
  9.4 0.0 all-gather.3.cloned.1.call-update
  9.4 0.0 all-gather.5.cloned.1.call-start
  9.5 0.7 all-gather.5.cloned.1.call-update
  10.2 0.0 reduce-scatter.2.cloned.1.call-start
  10.2 147.8 %all-gather.3.cloned.1.call-done = f32[32,512,128]{1,2,0:T(8,128)} async-done(((f32[32,128,128]{1,2,0:T(8,128)}), f32[32,512,128]{1,2,0:T(8,128)}) %all-gather.3.cloned.1.call-update) | async-done | bytes 8388624 | tf_op jit(solution)/shard_map/all_gather | solution.py:33
  158.0 1.8 fusion.26
  159.8 1.3 collective-permute-start
  161.1 1.3 collective-permute-start.1
  162.4 35.8 %all-gather.5.cloned.1.call-done = f32[9,512,256]{2,1,0:T(8,128)} async-done(((f32[9,128,256]{2,1,0:T(8,128)}), f32[9,512,256]{2,1,0:T(8,128)}) %all-gather.5.cloned.1.call-update) | async-done | bytes 4718608 | tf_op jit(solution)/shard_map/all_gather | solution.py:39
  198.2 9.8 %fusion.23 = f32[32,128,256]{2,1,0:T(8,128)S(1)} fusion(f32[32,512,128]{1,2,0:T(8,128)} %all-gather.3.cloned.1.call-done, f32[9,512,256]{2,1,0:T(8,128)} %all-gather.5.cloned.1.call-done), kind=kOutput, calls=%fused_computation.32 | convolution fusion | flops 6442450944 | bytes 13107200 | tf_op jit(solution)/shard_map/ric,io->roc/dot_general | solution.py:26
  208.1 8.3 %fusion.5 = f32[32,128,256]{2,1,0:T(8,128)} fusion(f32[1,512,128]{1,2,0:T(8,128)S(1)} %collective-permute-done.1, f32[32,512,128]{1,2,0:T(8,128)S(1)} %copy-done.1, f32[9,512,256]{2,1,0:T(8,128)S(1)} %copy-done.2), kind=kOutput, calls=%fused_computation.9 | convolution fusion | flops 6444613632 | bytes 13369344 | tf_op jit(solution)/shard_map/ric,io->roc/dot_general | solution.py:26
  216.4 8.3 %fusion.1 = f32[32,128,256]{2,1,0:T(8,128)} fusion(f32[32,512,128]{1,2,0:T(8,128)S(1)} %copy-done.1, f32[1,512,128]{1,2,0:T(8,128)S(1)} %collective-permute-done, f32[9,512,256]{2,1,0:T(8,128)S(1)} %copy-done.2), kind=kOutput, calls=%fused_computation.5 | convolution fusion | flops 6444613632 | bytes 13369344 | tf_op jit(solution)/shard_map/ric,io->roc/dot_general | solution.py:26
  224.7 1.8 select_maximum_fusion
  226.6 8.5 %fusion.11 = f32[32,128,256]{2,1,0:T(8,128)} fusion(f32[34,512,130]{1,2,0:T(8,128)S(1)} %select_maximum_fusion, f32[9,512,256]{2,1,0:T(8,128)S(1)} %copy-done.2), kind=kOutput, calls=%fused_computation.15 | convolution fusion | flops 6442450944 | bytes 13107200 | tf_op jit(solution)/shard_map/ric,io->roc/dot_general | solution.py:26
  235.1 8.4 %fusion.13 = f32[32,128,256]{2,1,0:T(8,128)} fusion(f32[34,512,130]{1,2,0:T(8,128)S(1)} %select_maximum_fusion, f32[9,512,256]{2,1,0:T(8,128)S(1)} %copy-done.2), kind=kOutput, calls=%fused_computation.17 | convolution fusion | flops 6442450944 | bytes 13107200 | tf_op jit(solution)/shard_map/ric,io->roc/dot_general | solution.py:26
  243.4 8.3 %fusion.15 = f32[32,128,256]{2,1,0:T(8,128)} fusion(f32[34,512,130]{1,2,0:T(8,128)S(1)} %select_maximum_fusion, f32[9,512,256]{2,1,0:T(8,128)S(1)} %copy-done.2), kind=kOutput, calls=%fused_computation.19 | convolution fusion | flops 6442450944 | bytes 13107200 | tf_op jit(solution)/shard_map/ric,io->roc/dot_general | solution.py:26
  251.7 8.4 %fusion.17 = f32[32,128,256]{2,1,0:T(8,128)} fusion(f32[34,512,130]{1,2,0:T(8,128)S(1)} %select_maximum_fusion, f32[9,512,256]{2,1,0:T(8,128)S(1)} %copy-done.2), kind=kOutput, calls=%fused_computation.21 | convolution fusion | flops 6442450944 | bytes 13107200 | tf_op jit(solution)/shard_map/ric,io->roc/dot_general | solution.py:26
  260.2 8.3 %fusion.19 = f32[32,128,256]{2,1,0:T(8,128)} fusion(f32[34,512,130]{1,2,0:T(8,128)S(1)} %select_maximum_fusion, f32[9,512,256]{2,1,0:T(8,128)S(1)} %copy-done.2), kind=kOutput, calls=%fused_computation.23 | convolution fusion | flops 6442450944 | bytes 13107200 | tf_op jit(solution)/shard_map/ric,io->roc/dot_general | solution.py:26
  268.5 18.4 %add_bitcast_fusion = f32[32,256,128]{1,2,0:T(8,128)} fusion(f32[32,128,256]{2,1,0:T(8,128)} %fusion.5, f32[32,128,256]{2,1,0:T(8,128)} %fusion.11, f32[32,128,256]{2,1,0:T(8,128)} %fusion.13, f32[32,128,256]{2,1,0:T(8,128)S(1)} %fusion.23, f32[32,128,256]{2,1,0:T(8,128)} %fusion.15, f32[32,128,256]{2,1,0:T(8,128)} %fusion.17, f32[32,128,256]{2,1,0:T(8,128)} %fusion.19, ...), kind=kOutput, calls=%fused_computation.25 | convolution fusion | flops 6450839552 | bytes 46661632 | tf_op jit(solution)/shard_map/ric,io->roc/dot_general | solution.py:26
  286.9 0.0 reduce-scatter.2.cloned.1.call-update
  286.9 53.5 %reduce-scatter.2.cloned.1.call-done = f32[32,128,128]{1,2,0:T(8,128)} async-done(((f32[32,256,128]{1,2,0:T(8,128)}), f32[32,128,128]{1,2,0:T(8,128)}) %reduce-scatter.2.cloned.1.call-update) | async-done | bytes 2097168 | tf_op jit(solution)/shard_map/reduce_scatter | solution.py:41
  340.4 1.7 broadcast_maximum_fusion
  342.2 1.8 copy.4
  (9 shorter events, 0.0 us)
Async XLA Ops:
  6.5 151.5 %all-gather.3.cloned.1.call-start = ((), (), s32[]{:S(2)}) async-start(), calls=%async_computation.1 | async-start | bytes 10485760 | tf_op jit(solution)/shard_map/all_gather | solution.py:33
  9.4 188.8 %all-gather.5.cloned.1.call-start = ((), (), s32[]{:S(2)}) async-start(), calls=%async_computation.2 | async-start | bytes 5898240 | tf_op jit(solution)/shard_map/all_gather | solution.py:39
  10.2 330.2 %reduce-scatter.2.cloned.1.call-start = ((), (), s32[]{:S(2)}) async-start(), calls=%async_computation.3 | async-start | bytes 6291456 | tf_op jit(solution)/shard_map/reduce_scatter | solution.py:41
  159.8 56.6 %collective-permute-start = (f32[1,512,128]{1,2,0:T(8,128)S(1)}, f32[1,512,128]{1,2,0:T(8,128)S(1)}, u32[]{:S(2)}, u32[]{:S(2)}) collective-permute-start(f32[1,512,128]{1,2,0:T(8,128)S(1)} %get-tuple-element.5), channel_id=1, source_target_pairs={{0,8},{8,16},{16,24},{1,9},{9,17},{17,25},{2,10},{10,18},{18,26},{... | collective-permute-start | bytes 786440 | tf_op jit(solution)/shard_map/ppermute | solution.py:12
  161.1 47.0 %collective-permute-start.1 = (f32[1,512,128]{1,2,0:T(8,128)}, f32[1,512,128]{1,2,0:T(8,128)S(1)}, u32[]{:S(2)}, u32[]{:S(2)}) collective-permute-start(f32[1,512,128]{1,2,0:T(8,128)} %get-tuple-element.6), channel_id=1, source_target_pairs={{8,0},{16,8},{24,16},{9,1},{17,9},{25,17},{10,2},{18,10},{26,18},{... | collective-permute-start | bytes 786440 | tf_op jit(solution)/shard_map/ppermute | solution.py:15
  198.2 9.9 %copy-start.1 = (f32[32,512,128]{1,2,0:T(8,128)S(1)}, f32[32,512,128]{1,2,0:T(8,128)}, u32[]{:S(2)}) copy-start(f32[32,512,128]{1,2,0:T(8,128)} %all-gather.3.cloned.1.call-done) | copy-start | bytes 25165828
  198.2 9.9 %copy-start.2 = (f32[9,512,256]{2,1,0:T(8,128)S(1)}, f32[9,512,256]{2,1,0:T(8,128)}, u32[]{:S(2)}) copy-start(f32[9,512,256]{2,1,0:T(8,128)} %all-gather.5.cloned.1.call-done) | copy-start | bytes 14155780
  226.6 33.6 %copy-start = (f32[34,512,130]{1,2,0:T(8,128)}, f32[34,512,130]{1,2,0:T(8,128)S(1)}, u32[]{:S(2)}) copy-start(f32[34,512,130]{1,2,0:T(8,128)S(1)} %select_maximum_fusion) | copy-start | bytes 27156484
Sparse Core Ops, SparseCore 0:
  9.6 148.4 all-gather.2
  159.6 38.5 all-gather.4
  287.0 53.3 reduce-scatter.1
where the time goes:
time: 352 us; the launch traced here: 350 us
  waiting for transfers between devices  238 us (68%)
  matrix products  86.7 us (25%)
  between operations  13.2 us (4%)
  local copies, waits for them, and re-layouts  6.47 us (2%)
  other arithmetic  3.58 us (1%)
    all_gather x1, waiting for transfers between devices, body(): panel = lax.all_gather(activations, 'filt', axis=1, tiled=True)  148 us
    dot_general x9, matrix products, convolve(): jnp.einsum('ric,io->roc', window, weights[tap_index], precision=lax.Preci...  86.7 us
    reduce_scatter x1, waiting for transfers between devices, body(): reduced = lax.psum_scatter(summed, 'layer', scatter_dimension=1, tiled=True)  53.5 us
    all_gather x1, waiting for transfers between devices, body(): gathered = lax.all_gather(filters, 'pos', axis=1, tiled=True)  35.8 us
  transfers between devices with their start and end apart: 5, of which 3 were waited for; matrix products, arithmetic and copies ran while one was open for 6% of the time, Pallas kernels for 0%

commit v1 on v0

v1 whole, which is shorter than its diff:
```python
import functools

import jax
import jax.numpy as jnp
from jax import lax
from jax.experimental import pallas as pl
from jax.experimental.pallas import tpu as pltpu
from jax.sharding import PartitionSpec as P

VMEM_BYTES = 48 << 20
APART = False
SHARES = (5, 5, 4, 2)
DEPTHS = (2, 2, 2)
FACTOR = 1.0
EFFORT = 0.0


def split(value):
    high = value.astype(jnp.bfloat16)
    low = (value - high.astype(jnp.float32)).astype(jnp.bfloat16)
    return high, low


def prepare_kernel(place_ref, *refs):
    pieces, (high_ref, low_ref) = refs[:-2], refs[-2:]
    for index, piece in enumerate(pieces):
        depth, wide = piece.shape[1:]
        high, low = split(piece[0].T)
        half = wide // 2
        columns = slice(None)
        if len(pieces) > 1:
            columns = pl.ds(pl.multiple_of(place_ref[1 + index] * depth, depth), depth)
        for side in range(2):
            rows = place_ref[0] * half if side else (1 - place_ref[0]) * half
            rows = pl.ds(pl.multiple_of(rows, half), half)
            source = slice(side * half, (side + 1) * half)
            high_ref[0, rows, columns] = high[source]
            low_ref[0, rows, columns] = low[source]


def prepare(pieces, place):
    wide = pieces[0].shape[2]
    depth = sum(piece.shape[1] for piece in pieces)
    shape = jax.ShapeDtypeStruct((3, 3 * wide, depth), jnp.bfloat16)
    block = pl.BlockSpec((1, wide, depth), lambda t, s: (t // 3, t % 3, 0))
    return pl.pallas_call(
        prepare_kernel,
        out_shape=(shape, shape),
        grid_spec=pltpu.PrefetchScalarGridSpec(
            num_scalar_prefetch=1,
            grid=(9,),
            in_specs=[pl.BlockSpec((1,) + piece.shape[1:], lambda t, s: (t, 0, 0)) for piece in pieces],
            out_specs=(block, block),
        ),
        compiler_params=pltpu.CompilerParams(vmem_limit_bytes=VMEM_BYTES),
        cost_estimate=pl.CostEstimate(flops=1000 + int(EFFORT * 1e9), bytes_accessed=1000, transcendentals=0),
    )(place, *pieces)


def conv_kernel(sources, ahead, pairs, start, end, parts, place_ref, *refs):
    size = 1 + max(index for group in sources + ahead for index in group)
    arrays, refs = refs[:size], refs[size:]
    before, high_w, low_w = refs[:3]
    results, tail, high_x, low_x = refs[3 : 3 + len(parts)], refs[3 + len(parts)], *refs[4 + len(parts) :]
    channels, across = arrays[0].shape[1:]
    wide = high_w.shape[1] // 3
    half = wide // 2

    def put(side, row, slot, value):
        high, low = split(value)
        rows = pl.ds(pl.multiple_of(place_ref[slot] * channels, channels), channels)
        high_x[side, row, rows, :] = high
        low_x[side, row, rows, :] = low

    def put_rows(groups, first, many):
        for slot, group in enumerate(groups):
            for row in range(many):
                for side in range(2):
                    from_row = arrays[group[0]].shape[0] - 1 - row if side else row
                    value = arrays[group[0]][from_row]
                    for index in group[1:]:
                        value = value + arrays[index][from_row]
                    put(side, first + row, slot, value)

    if start == "halo":
        for side in range(2):
            for slot in range(len(sources)):
                put(side, 0, slot, before[side, slot])
    elif start == "tail":
        for side in range(2):
            for row in range(2):
                high_x[side, row] = before[0, side, row]
                low_x[side, row] = before[1, side, row]
    base = STARTS[start]
    total = base + pairs
    put_rows(sources, base, pairs)
    for side in range(2):
        for row in range(2):
            tail[0, side, row] = high_x[side, total - 2 + row]
            tail[1, side, row] = low_x[side, total - 2 + row]
    if end == "meet":
        for side in range(2):
            high_x[side, total] = high_x[1 - side, total - 1]
            low_x[side, total] = low_x[1 - side, total - 1]
    elif end == "ahead":
        put_rows(ahead, total, 2)
    outs = total + ENDS[end] - 2
    taken = half * len(parts)
    lane = lax.broadcasted_iota(jnp.int32, (taken, across), 1)

    def rows_of(ref, a):
        if len(parts) == 2:
            return ref[a]
        return jnp.concatenate([ref[a, pl.ds(b * wide + parts[0] * half, half)] for b in range(3)], axis=0)

    def step(q, carry):
        total_sum = None
        for a in range(3):
            high = jnp.concatenate([high_x[0, q + a], high_x[1, q + 2 - a]], axis=1)
            low = jnp.concatenate([low_x[0, q + a], low_x[1, q + 2 - a]], axis=1)
            dot = functools.partial(jnp.dot, preferred_element_type=jnp.float32)
            high_rows, low_rows = rows_of(high_w, a), rows_of(low_w, a)
            part = dot(high_rows, high) + dot(high_rows, low) + dot(low_rows, high)
            total_sum = part if total_sum is None else total_sum + part
        for side in range(2):
            lanes = slice(side * across, (side + 1) * across)
            left = pltpu.roll(total_sum[:taken, lanes], 1, 1)
            right = pltpu.roll(total_sum[2 * taken :, lanes], across - 1, 1)
            result = (
                total_sum[taken : 2 * taken, lanes]
                + jnp.where(lane == 0, 0.0, left)
                + jnp.where(lane == across - 1, 0.0, right)
            )
            row = q if side == 0 else outs - 1 - q
            for index, ref in enumerate(results):
                ref[side, row] = result[index * half : (index + 1) * half]
        return carry

    lax.fori_loop(0, outs, step, 0)


STARTS = {"none": 0, "halo": 1, "tail": 2}
ENDS = {"none": 0, "meet": 1, "ahead": 2}


def conv(place, groups, before, weights, pairs, start, end, ahead, parts):
    arrays, numbers = [], []
    for group in list(groups) + list(ahead):
        numbers.append(tuple(range(len(arrays), len(arrays) + len(group))))
        arrays += group
    sources, ahead = tuple(numbers[: len(groups)]), tuple(numbers[len(groups) :])
    channels, across = arrays[0].shape[1:]
    depth = channels * len(groups)
    wide = weights[0].shape[1] // 3
    rows = STARTS[start] + pairs + ENDS[end]
    outs = rows - 2
    result = jax.ShapeDtypeStruct((2, outs, wide // 2, across), jnp.float32)
    tail = jax.ShapeDtypeStruct((2, 2, 2, depth, across), jnp.bfloat16)
    vmem = pl.BlockSpec(memory_space=pltpu.VMEM)
    flops = 2 * 2 * outs * across * 9 * depth * wide * 3 * len(parts) // 2
    return pl.pallas_call(
        functools.partial(conv_kernel, sources, ahead, pairs, start, end, parts),
        out_shape=(result,) * len(parts) + (tail,),
        in_specs=[pl.BlockSpec(memory_space=pltpu.SMEM)] + [vmem] * (len(arrays) + 3),
        out_specs=(vmem,) * (len(parts) + 1),
        scratch_shapes=[
            pltpu.VMEM((2, rows, depth, across), jnp.bfloat16),
            pltpu.VMEM((2, rows, depth, across), jnp.bfloat16),
        ],
        compiler_params=pltpu.CompilerParams(vmem_limit_bytes=VMEM_BYTES),
        cost_estimate=pl.CostEstimate(flops=1000 + int(flops * FACTOR), bytes_accessed=1000, transcendentals=0),
    )(place, *arrays, before, *weights)


class Cell:
    def __init__(self, value):
        self.value = value


def after(value, cells):
    cells = [cell for cell in cells if cell is not None]
    if not cells:
        return value
    value, *others = lax.optimization_barrier((value, *(cell.value for cell in cells)))
    for cell, other in zip(cells, others):
        cell.value = other
    return value


class Lane:
    def __init__(self, axis, most=2):
        self.axis, self.most, self.sent = axis, most, []

    def send(self, value, pairs, *cells):
        held = self.sent[-self.most] if len(self.sent) >= self.most else None
        cell = Cell(lax.ppermute(after(value, (held,) + cells), self.axis, pairs))
        self.sent.append(cell)
        return cell


def edges(count, step, parity, ends):
    moves = []
    for low in range(parity, count - 1, 2):
        if low >= step and (ends or low + 1 < count - 1):
            moves.append((low, low + 1))
        if low + 1 <= count - 1 - step and (ends or low > 0):
            moves.append((low + 1, low))
    return moves


def gathered(piece, lane, cells=()):
    count = lax.axis_size("pos")
    pieces = {0: Cell(piece)}
    bit = count // 2
    while bit:
        swap = [(i, i ^ bit) for i in range(count)]
        pieces.update({key ^ bit: lane.send(cell.value, swap, *cells) for key, cell in list(pieces.items())})
        bit //= 2
    return pieces


def chunk_sizes(half):
    total = sum(SHARES)
    return [half * share // total for share in SHARES] if half % total == 0 else [half]


ORDER = (('E00',), ('O00',), ('E10',), ('O01',), ('E01',), ('O10',), ('E02',), ('O11',), ('E12', 'E01'), ('E11',), ('O20',), ('H', 'O20'), ('P',), ('K0', 'E11'), ('E20', 'X3'), ('O21',), ('E21',), ('K1',), ('E30',), ('O30',), ('E22',), ('O31', 'E20'), ('E31',), ('K2', 'Y0', 'E22'), ('E32',), ('K3',))


def body(activations, filters):
    count = lax.axis_size("filt")
    me = lax.axis_index("filt")
    layer = lax.axis_index("layer")
    position, positions = lax.axis_index("pos"), lax.axis_size("pos")
    height, channels, across = activations.shape
    half = height // 2
    apart = APART and count >= 4 and half % sum(SHARES) == 0
    forward = [(i, i + 1) for i in range(positions - 1)]
    backward = [(i + 1, i) for i, _ in forward]
    swap = [(0, 1), (1, 0)]

    sizes = chunk_sizes(half)
    starts = [sum(sizes[:i]) for i in range(len(sizes))]
    chunks = [
        jnp.concatenate([activations[s : s + m], activations[height - s - m : height - s]], axis=0)
        for s, m in zip(starts, sizes)
    ]
    lanes = {"E": Lane("filt", DEPTHS[0]), "O": Lane("filt", DEPTHS[1]), "W": Lane("filt"), "Y": Lane("layer", DEPTHS[2])}
    lanes["X"] = Lane("pos", 99)
    by_swaps = positions & (positions - 1) == 0 and filters.shape[1] % 128 == 0
    turn = 1 - 2 * (me % 2)
    place = jnp.mod(me + turn * jnp.arange(count), count).astype(jnp.int32)
    order = layer.astype(jnp.int32).reshape(1)
    if by_swaps:
        keys = gathered_keys(positions)
        order = jnp.concatenate([order, jnp.stack([position ^ key for key in keys]).astype(jnp.int32)])
    cells = {}

    def spread(name, piece, waits=()):
        if not by_swaps:
            cells[name + "0"] = Cell(lax.all_gather(piece, "pos", axis=1, tiled=True))
            return
        pieces = gathered(piece, lanes["X"], waits)
        cells.update({name + str(index): pieces[key] for index, key in enumerate(keys)})

    def prepared(name):
        pieces = [cells[key].value for key in sorted(cells) if key[0] == name]
        return [Cell(array) for array in prepare(pieces, order)]

    def move(word, waits):
        kind, index, step = word[0], int(word[1]), int(word[2])
        ends = index > 0 or not apart
        source = Cell(chunks[index]) if step == 0 else cells.get("OE"["EO".index(kind)] + f"{index}{step - 1}")
        moves = edges(count, step, "EO".index(kind), ends)
        if moves and source is not None:
            lane = "W" if kind == "E" and not ends else kind
            cells[word] = lanes[lane].send(source.value, moves, *waits)

    def groups(index):
        result = [[chunks[index]]]
        for slot in range(1, count):
            words = [f"E{index}{slot - 1}"] + ([f"O{index}{count - 1 - slot}"] if slot >= 2 else [])
            result.append([cells[word].value for word in words if word in cells])
        return result

    def halo():
        parts = groups(0)
        above, below = (
            jnp.stack([sum(array[row] for array in part) for part in parts]) for row in (2 * sizes[0] - 1, 0)
        )
        return Cell(jnp.stack([lax.ppermute(above, "pos", forward), lax.ppermute(below, "pos", backward)]))

    tails = {}

    def compute(kind, index, waits, parts=(0, 1)):
        first, last = index == 0, index == len(chunks) - 1
        if first:
            before, start = cells["H"].value, "halo"
        elif index == 1 and apart:
            before, start = order, "none"
        else:
            before, start = tails[index - 1], "tail"
        end, ahead = "meet" if last else "none", ()
        if first and apart:
            end, ahead = "ahead", groups(1)
        weights = [cell.value for cell in (own_weights if kind == "K" else end_weights)]
        before = after(before, waits)
        *results, tails[index] = conv(
            place, groups(index), before, weights, sizes[index], start, end, ahead, parts
        )
        if 1 in parts:
            cells[f"{kind}{index}"] = Cell(results[-1])
        if 0 in parts:
            cells[("Y" if kind == "K" else "Z") + str(index)] = lanes["Y"].send(results[0], swap)

    def total(kind, index):
        other = cells[("Y" if kind == "K" else "Z") + str(index)]
        return jnp.maximum(cells[f"{kind}{index}"].value + other.value, 0.0)

    first = Cell(chunks[0])
    spread("X", after(filters, [first]))
    chunks[0] = first.value
    if len(chunks) > 1 and count == 4:
        plan = ORDER
    else:
        plan = [("W",), ("P",), ("Q",)]
        for index in range(len(chunks)):
            for step in range(count - 1):
                plan += [(f"E{index}{step}",)] + ([(f"O{index}{step}",)] if step < count - 2 else [])
        plan += [("H",)] + [(f"K{index}",) for index in range(len(chunks))] + [("L0",), ("S",)]
    for word, *names in plan:
        kind = word[0]
        waits = [cells[name] for name in names if name in cells]
        if kind in "EO":
            move(word, waits)
        elif kind == "H":
            cells["H"] = halo()
        elif kind == "P":
            own_weights = prepared("X")
            cells["P"] = own_weights[0]
        elif kind == "K":
            compute(kind, int(word[1]), waits)
        elif kind in "AB":
            compute("K", int(word[1]), waits, ("AB".index(kind),))
        elif not apart:
            continue
        elif kind == "L":
            compute(kind, int(word[1]), waits)
        elif kind == "W":
            cells["W"] = lanes["W"].send(filters, [(0, 1), (count - 1, count - 2)], *waits)
            spread("V", cells["W"].value, [cells[name] for name in ("X1",) if name in cells])
        elif kind == "Q":
            end_weights = prepared("V")
            cells["Q"] = end_weights[0]
        elif kind == "S":
            result = after(total("L", 0), waits)
            cells["S"] = lanes["E"].send(result, [(1, 0), (count - 2, count - 1)])
    blocks = [total("K", index) for index in range(len(chunks))]
    if apart:
        at_end = (me == 0) | (me == count - 1)
        blocks[0] = jnp.where(at_end, cells["S"].value, blocks[0])
    return jnp.concatenate([block[0] for block in blocks] + [block[1] for block in reversed(blocks)], axis=0)


def gathered_keys(positions):
    keys = [0]
    bit = positions // 2
    while bit:
        keys += [key ^ bit for key in keys]
        bit //= 2
    return keys


def solution(mesh):
    in_specs = (P("pos", ("layer", "filt"), None), P(None, ("layer", "pos"), "filt"))
    out_specs = P("pos", ("filt", "layer"), None)
    return jax.shard_map(body, mesh=mesh, in_specs=in_specs, out_specs=out_specs, check_vma=False)
```

time: 352 us -> 177 us (0.50)
  waiting for transfers between devices: 238 us -> 60.6 us
  matrix products: 86.7 us -> 0 us
  Pallas kernels: 0 us -> 53.9 us
  starting transfers between devices: 2.67 us -> 48.9 us
  between operations: 13.2 us -> 0.64 us
    all_gather x2 -> x0, waiting for transfers between devices: 184 us -> none  [the longest x1 148 us: body(): panel = lax.all_gather(activations, 'filt', axis=1, tiled=True)]
    dot_general x9 -> x0, matrix products: 86.7 us -> none  [convolve(): jnp.einsum('ric,io->roc', window, weights[tap_index], precision=lax.Preci...]
    ppermute x2 -> x29, waiting for transfers between devices: 0.01 us -> 60.6 us  [the longest x27 59.4 us: send(): cell = Cell(lax.ppermute(after(value, (held,) + cells), self.axis, pairs))]
    pallas_call x0 -> x5, Pallas kernels: none -> 53.9 us  [the longest x4 45.9 us: conv(): pl.pallas_call(functools.partial(conv_kernel, sources, ahead, pairs, star...]
    reduce_scatter x1 -> x0, waiting for transfers between devices: 53.5 us -> none  [body(): reduced = lax.psum_scatter(summed, 'layer', scatter_dimension=1, tiled=True)]
    ppermute x2 -> x29, starting transfers between devices: 2.59 us -> 48.9 us  [the longest x27 45.6 us: send(): cell = Cell(lax.ppermute(after(value, (held,) + cells), self.axis, pairs))]
  transfers between devices with their start and end apart: 5 -> 29, of which waited for: 3 -> 11; matrix products, arithmetic and copies ran while one was open for 6% -> 3% of each run, Pallas kernels for 0% -> 31%
where the time goes in v1:
time: 177 us; the launch traced here: 176 us
  waiting for transfers between devices  60.6 us (34%)
  Pallas kernels  53.9 us (30%)
  starting transfers between devices  48.9 us (28%)
  local copies, waits for them, and re-layouts  8.33 us (5%)
  other arithmetic  3.74 us (2%)
    ppermute x27, waiting for transfers between devices, send(): cell = Cell(lax.ppermute(after(value, (held,) + cells), self.axis, pairs))  59.4 us
    pallas_call x4, Pallas kernels, conv(): pl.pallas_call(functools.partial(conv_kernel, sources, ahead, pairs, star...  45.9 us
    ppermute x27, starting transfers between devices, send(): cell = Cell(lax.ppermute(after(value, (held,) + cells), self.axis, pairs))  45.6 us
    pallas_call x1, Pallas kernels, prepare(): pl.pallas_call(prepare_kernel, out_shape=(shape, shape), grid_spec=pltpu....  8.06 us
    unnamed x53, local copies, waits for them, and re-layouts  4.16 us
  transfers between devices with their start and end apart: 29, of which 11 were waited for; matrix products, arithmetic and copies ran while one was open for 3% of the time, Pallas kernels for 31%

profile of v1, /device:TPU:16, one launch (start us, length us, event | category | flops | bytes accessed | tf_op | source)
XLA Modules:
  0.0 176.2 jit_solution(10713008636799969752)
XLA Ops:
  6.7 12.5 %collective-permute-done.1.refs_1_ = f32[10,128,128]{2,1,0:T(8,128)S(1)} collective-permute-done((f32[10,128,128]{2,1,0:T(8,128)S(1)}, f32[10,128,128]{2,1,0:T(8,128)S(1)}, u32[]{:S(2)}, u32[]{:S(2)}) %collective-permute-start.1) | collective-permute-done | bytes 655392 | tf_op jit(solution)/shard_map/ppermute | solution.py:196
  19.2 2.3 %collective-permute-start.2 = (f32[10,128,128]{2,1,0:T(8,128)S(1)}, f32[10,128,128]{2,1,0:T(8,128)S(1)}, u32[]{:S(2)}, u32[]{:S(2)}) collective-permute-start(f32[10,128,128]{2,1,0:T(8,128)S(1)} %collective-permute-done.1.refs_1_), channel_id=1, source_target_pairs={{2,4},{4,2},{3,5},{5,3},{10,12},{12,10},{11,13},{13,11},{18,20},{2... | collective-permute-start | bytes 1966088 | tf_op jit(solution)/shard_map/ppermute | solution.py:196
  24.7 7.7 %collective-permute-done.3.refs_1_ = f32[10,128,128]{2,1,0:T(8,128)S(1)} collective-permute-done((f32[10,128,128]{2,1,0:T(8,128)S(1)}, f32[10,128,128]{2,1,0:T(8,128)S(1)}, u32[]{:S(2)}, u32[]{:S(2)}) %collective-permute-start.3) | collective-permute-done | bytes 655392 | tf_op jit(solution)/shard_map/ppermute | solution.py:196
  32.4 4.2 %collective-permute-done.2.refs_3_ = f32[10,128,128]{2,1,0:T(8,128)S(1)} collective-permute-done((f32[10,128,128]{2,1,0:T(8,128)S(1)}, f32[10,128,128]{2,1,0:T(8,128)S(1)}, u32[]{:S(2)}, u32[]{:S(2)}) %collective-permute-start.2) | collective-permute-done | bytes 655392 | tf_op jit(solution)/shard_map/ppermute | solution.py:196
  36.5 2.2 %collective-permute-start.4 = (f32[10,128,128]{2,1,0:T(8,128)S(1)}, f32[10,128,128]{2,1,0:T(8,128)S(1)}, u32[]{:S(2)}, u32[]{:S(2)}) collective-permute-start(f32[10,128,128]{2,1,0:T(8,128)S(1)} %collective-permute-done.3.refs_1_), channel_id=1, source_target_pairs={{2,4},{4,2},{3,5},{5,3},{10,12},{12,10},{11,13},{13,11},{18,20},{2... | collective-permute-start | bytes 1966088 | tf_op jit(solution)/shard_map/ppermute | solution.py:196
  39.6 3.6 %collective-permute-start.6 = (f32[10,128,128]{2,1,0:T(8,128)S(1)}, f32[10,128,128]{2,1,0:T(8,128)}, u32[]{:S(2)}, u32[]{:S(2)}) collective-permute-start(f32[10,128,128]{2,1,0:T(8,128)S(1)} %pad_maximum_fusion.1.refs_0_), channel_id=1, source_target_pairs={{2,4},{4,2},{3,5},{5,3},{10,12},{12,10},{11,13},{13,11},{18,20},{2... | collective-permute-start | bytes 1966088 | tf_op jit(solution)/shard_map/ppermute | solution.py:196
  48.0 8.1 %collective-permute-done.4.refs_3_ = f32[10,128,128]{2,1,0:T(8,128)S(1)} collective-permute-done((f32[10,128,128]{2,1,0:T(8,128)S(1)}, f32[10,128,128]{2,1,0:T(8,128)S(1)}, u32[]{:S(2)}, u32[]{:S(2)}) %collective-permute-start.4) | collective-permute-done | bytes 655392 | tf_op jit(solution)/shard_map/ppermute | solution.py:196
  58.2 8.8 %collective-permute-done.6.refs_5_ = f32[10,128,128]{2,1,0:T(8,128)} collective-permute-done((f32[10,128,128]{2,1,0:T(8,128)S(1)}, f32[10,128,128]{2,1,0:T(8,128)}, u32[]{:S(2)}, u32[]{:S(2)}) %collective-permute-start.6) | collective-permute-done | bytes 655392 | tf_op jit(solution)/shard_map/ppermute | solution.py:196
  67.0 2.2 %collective-permute-start.18 = (f32[8,128,128]{2,1,0:T(8,128)}, f32[8,128,128]{2,1,0:T(8,128)}, u32[]{:S(2)}, u32[]{:S(2)}) collective-permute-start(f32[8,128,128]{2,1,0:T(8,128)} %pad_maximum_fusion.3.refs_0_), channel_id=1, source_target_pairs={{2,4},{4,2},{3,5},{5,3},{10,12},{12,10},{11,13},{13,11},{18,20},{2... | collective-permute-start | bytes 1572872 | tf_op jit(solution)/shard_map/ppermute | solution.py:196
  69.3 2.2 %collective-permute-start.10 = (f32[10,128,128]{2,1,0:T(8,128)}, f32[10,128,128]{2,1,0:T(8,128)}, u32[]{:S(2)}, u32[]{:S(2)}) collective-permute-start(f32[10,128,128]{2,1,0:T(8,128)} %collective-permute-done.6.refs_5_), channel_id=1, source_target_pairs={{2,0},{4,6},{3,1},{5,7},{10,8},{12,14},{11,9},{13,15},{18,16},{20,... | collective-permute-start | bytes 1966088 | tf_op jit(solution)/shard_map/ppermute | solution.py:196
  71.5 2.4 %collective-permute-done.14.refs_4_ = f32[10,128,128]{2,1,0:T(8,128)S(1)} collective-permute-done((f32[10,128,128]{2,1,0:T(8,128)S(1)}, f32[10,128,128]{2,1,0:T(8,128)S(1)}, u32[]{:S(2)}, u32[]{:S(2)}) %collective-permute-start.14) | collective-permute-done | bytes 655392 | tf_op jit(solution)/shard_map/ppermute | solution.py:196
  74.7 2.5 %collective-permute-start.15 = (f32[8,128,128]{2,1,0:T(8,128)}, f32[8,128,128]{2,1,0:T(8,128)}, u32[]{:S(2)}, u32[]{:S(2)}) collective-permute-start(f32[8,128,128]{2,1,0:T(8,128)} %pad_maximum_fusion.3.refs_0_), channel_id=1, source_target_pairs={{0,2},{2,0},{4,6},{6,4},{1,3},{3,1},{5,7},{7,5},{8,10},{10,8},{12,... | collective-permute-start | bytes 1572872 | tf_op jit(solution)/shard_map/ppermute | solution.py:196
  82.2 2.2 %collective-permute-start.22 = (f32[4,128,128]{2,1,0:T(8,128)}, f32[4,128,128]{2,1,0:T(8,128)S(1)}, u32[]{:S(2)}, u32[]{:S(2)}) collective-permute-start(f32[4,128,128]{2,1,0:T(8,128)} %get-tuple-element.104.refs_0_), channel_id=1, source_target_pairs={{2,4},{4,2},{3,5},{5,3},{10,12},{12,10},{11,13},{13,11},{18,20},{2... | collective-permute-start | bytes 786440 | tf_op jit(solution)/shard_map/ppermute | solution.py:196
  86.8 8.1 %shard_map.28 = (bf16[3,768,512]{2,1,0:T(8,128)(2,1)}, bf16[3,768,512]{2,1,0:T(8,128)(2,1)}) custom-call(s32[5]{0:T(128)S(1)} %concatenate.20.place_ref, f32[9,128,256]{2,1,0:T(8,128)S(1)} %copy-done, f32[9,128,256]{2,1,0:T(8,128)S(1)} %collective-permute-done.11.refs_1_, f32[9,128,256]{2,1,0:T(8,128)} %collective-permute-done.12.refs_2_, ...), custom_call_target="tpu_custom_call" | custom-call | flops 1000 | bytes 1000 | tf_op jit(solution)/shard_map/pallas_call | solution.py:46
  96.8 2.2 %collective-permute-done.15.refs_1_ = f32[8,128,128]{2,1,0:T(8,128)} collective-permute-done((f32[8,128,128]{2,1,0:T(8,128)}, f32[8,128,128]{2,1,0:T(8,128)}, u32[]{:S(2)}, u32[]{:S(2)}) %collective-permute-start.15) | collective-permute-done | bytes 524320 | tf_op jit(solution)/shard_map/ppermute | solution.py:196
  99.0 2.2 %collective-permute-start.17 = (f32[8,128,128]{2,1,0:T(8,128)}, f32[8,128,128]{2,1,0:T(8,128)S(1)}, u32[]{:S(2)}, u32[]{:S(2)}) collective-permute-start(f32[8,128,128]{2,1,0:T(8,128)} %collective-permute-done.15.refs_1_), channel_id=1, source_target_pairs={{2,4},{4,2},{3,5},{5,3},{10,12},{12,10},{11,13},{13,11},{18,20},{2... | collective-permute-start | bytes 1572872 | tf_op jit(solution)/shard_map/ppermute | solution.py:196
  102.3 11.2 %shard_map.29 = (f32[2,4,128,128]{3,2,1,0:T(8,128)S(1)}, f32[2,4,128,128]{3,2,1,0:T(8,128)S(1)}, bf16[2,2,2,512,128]{4,3,2,1,0:T(8,128)(2,1)}) custom-call(s32[4]{0:T(128)S(1)} %and_select_fusion.place_ref, f32[10,128,128]{2,1,0:T(8,128)S(1)} %copy-done.2, f32[10,128,128]{2,1,0:T(8,128)S(1)} %copy-done.15, f32[10,128,128]{2,1,0:T(8,128)S(1)} %copy-done.11, ...), custom_call_target="tpu_custom_call" | custom-call | flops 7247758336 | bytes 1000 | tf_op jit(solution)/shard_map/pallas_call | solution.py:161
  115.2 3.0 %collective-permute-start.21 = (f32[8,128,128]{2,1,0:T(8,128)S(1)}, f32[8,128,128]{2,1,0:T(8,128)S(1)}, u32[]{:S(2)}, u32[]{:S(2)}) collective-permute-start(f32[8,128,128]{2,1,0:T(8,128)S(1)} %collective-permute-done.17.refs_3_), channel_id=1, source_target_pairs={{2,0},{4,6},{3,1},{5,7},{10,8},{12,14},{11,9},{13,15},{18,16},{20,... | collective-permute-start | bytes 1572872 | tf_op jit(solution)/shard_map/ppermute | solution.py:196
  118.2 3.6 %collective-permute-start.24 = (f32[4,128,128]{2,1,0:T(8,128)S(1)}, f32[4,128,128]{2,1,0:T(8,128)S(1)}, u32[]{:S(2)}, u32[]{:S(2)}) collective-permute-start(f32[4,128,128]{2,1,0:T(8,128)S(1)} %collective-permute-done.16.refs_1_), channel_id=1, source_target_pairs={{2,4},{4,2},{3,5},{5,3},{10,12},{12,10},{11,13},{13,11},{18,20},{2... | collective-permute-start | bytes 786440 | tf_op jit(solution)/shard_map/ppermute | solution.py:196
  121.8 13.9 %shard_map.30 = (f32[2,5,128,128]{3,2,1,0:T(8,128)S(1)}, f32[2,5,128,128]{3,2,1,0:T(8,128)S(1)}, bf16[2,2,2,512,128]{4,3,2,1,0:T(8,128)(2,1)}) custom-call(s32[4]{0:T(128)S(1)} %and_select_fusion.place_ref, f32[10,128,128]{2,1,0:T(8,128)S(1)} %copy-done.4, f32[10,128,128]{2,1,0:T(8,128)S(1)} %copy-done.17, f32[10,128,128]{2,1,0:T(8,128)} %collective-permute-done.10.refs_2_, ...), custom_call_target="tpu_custom_call" | custom-call | flops 9059697664 | bytes 1000 | tf_op jit(solution)/shard_map/pallas_call | solution.py:161
  139.0 11.8 %shard_map.31 = (f32[2,4,128,128]{3,2,1,0:T(8,128)S(1)}, f32[2,4,128,128]{3,2,1,0:T(8,128)S(1)}, bf16[2,2,2,512,128]{4,3,2,1,0:T(8,128)(2,1)S(1)}) custom-call(s32[4]{0:T(128)S(1)} %and_select_fusion.place_ref, f32[8,128,128]{2,1,0:T(8,128)} %pad_maximum_fusion.3.refs_0_, f32[8,128,128]{2,1,0:T(8,128)} %collective-permute-done.15.refs_1_, ...), custom_call_target="tpu_custom_call" | custom-call | flops 7247758336 | bytes 1000 | tf_op jit(solution)/shard_map/pallas_call | solution.py:161
  152.5 8.9 %shard_map.32 = (f32[2,3,128,128]{3,2,1,0:T(8,128)S(1)}, f32[2,3,128,128]{3,2,1,0:T(8,128)S(1)}, bf16[2,2,2,512,128]{4,3,2,1,0:T(8,128)(2,1)}) custom-call(s32[4]{0:T(128)S(1)} %and_select_fusion.place_ref, f32[4,128,128]{2,1,0:T(8,128)S(1)} %copy-done.5, f32[4,128,128]{2,1,0:T(8,128)S(1)} %collective-permute-done.16.refs_1_, ...), custom_call_target="tpu_custom_call" | custom-call | flops 5435819008 | bytes 1000 | tf_op jit(solution)/shard_map/pallas_call | solution.py:161
  162.1 3.5 %collective-permute-done.27 = f32[2,4,128,128]{3,2,1,0:T(8,128)S(1)} collective-permute-done((f32[2,4,128,128]{3,2,1,0:T(8,128)S(1)}, f32[2,4,128,128]{3,2,1,0:T(8,128)S(1)}, u32[]{:S(2)}, u32[]{:S(2)}) %collective-permute-start.27) | collective-permute-done | bytes 524320 | tf_op jit(solution)/shard_map/ppermute | solution.py:196
  165.8 8.3 %collective-permute-done.28 = f32[2,3,128,128]{3,2,1,0:T(8,128)S(1)} collective-permute-done((f32[2,3,128,128]{3,2,1,0:T(8,128)S(1)}, f32[2,3,128,128]{3,2,1,0:T(8,128)S(1)}, u32[]{:S(2)}, u32[]{:S(2)}) %collective-permute-start.28) | collective-permute-done | bytes 393248 | tf_op jit(solution)/shard_map/ppermute | solution.py:196
  (111 shorter events, 38.1 us)
Async XLA Ops:
  1.5 17.7 %collective-permute-start.1 = (f32[10,128,128]{2,1,0:T(8,128)S(1)}, f32[10,128,128]{2,1,0:T(8,128)S(1)}, u32[]{:S(2)}, u32[]{:S(2)}) collective-permute-start(f32[10,128,128]{2,1,0:T(8,128)S(1)} %pad_maximum_fusion.refs_0_), channel_id=1, source_target_pairs={{0,2},{2,0},{4,6},{6,4},{1,3},{3,1},{5,7},{7,5},{8,10},{10,8},{12,... | collective-permute-start | bytes 1966088 | tf_op jit(solution)/shard_map/ppermute | solution.py:196
  3.2 40.1 %collective-permute-start.11 = (f32[9,128,256]{2,1,0:T(8,128)S(1)}, f32[9,128,256]{2,1,0:T(8,128)S(1)}, u32[]{:S(2)}, u32[]{:S(2)}) collective-permute-start(f32[9,128,256]{2,1,0:T(8,128)S(1)} %copy-done), channel_id=1, source_target_pairs={{0,16},{8,24},{16,0},{24,8},{1,17},{9,25},{17,1},{25,9},{2,18},{10... | collective-permute-start | bytes 3538952 | tf_op jit(solution)/shard_map/ppermute | solution.py:196
  4.7 18.7 %collective-permute-start = (f32[10,128,128]{2,1,0:T(8,128)S(1)}, f32[10,128,128]{2,1,0:T(8,128)S(1)}, u32[]{:S(2)}, u32[]{:S(2)}) collective-permute-start(f32[10,128,128]{2,1,0:T(8,128)S(1)} %pad_maximum_fusion.refs_0_), channel_id=1, source_target_pairs={{2,4},{4,2},{3,5},{5,3},{10,12},{12,10},{11,13},{13,11},{18,20},{2... | collective-permute-start | bytes 1966088 | tf_op jit(solution)/shard_map/ppermute | solution.py:196
  6.7 25.7 %collective-permute-start.3 = (f32[10,128,128]{2,1,0:T(8,128)S(1)}, f32[10,128,128]{2,1,0:T(8,128)S(1)}, u32[]{:S(2)}, u32[]{:S(2)}) collective-permute-start(f32[10,128,128]{2,1,0:T(8,128)S(1)} %pad_maximum_fusion.1.refs_0_), channel_id=1, source_target_pairs={{0,2},{2,0},{4,6},{6,4},{1,3},{3,1},{5,7},{7,5},{8,10},{10,8},{12,... | collective-permute-start | bytes 1966088 | tf_op jit(solution)/shard_map/ppermute | solution.py:196
  19.2 17.3 %collective-permute-start.2 = (f32[10,128,128]{2,1,0:T(8,128)S(1)}, f32[10,128,128]{2,1,0:T(8,128)S(1)}, u32[]{:S(2)}, u32[]{:S(2)}) collective-permute-start(f32[10,128,128]{2,1,0:T(8,128)S(1)} %collective-permute-done.1.refs_1_), channel_id=1, source_target_pairs={{2,4},{4,2},{3,5},{5,3},{10,12},{12,10},{11,13},{13,11},{18,20},{2... | collective-permute-start | bytes 1966088 | tf_op jit(solution)/shard_map/ppermute | solution.py:196
  23.4 24.1 %collective-permute-start.5 = (f32[10,128,128]{2,1,0:T(8,128)S(1)}, f32[10,128,128]{2,1,0:T(8,128)S(1)}, u32[]{:S(2)}, u32[]{:S(2)}) collective-permute-start(f32[10,128,128]{2,1,0:T(8,128)S(1)} %collective-permute-done.refs_5_), channel_id=1, source_target_pairs={{2,0},{4,6},{3,1},{5,7},{10,8},{12,14},{11,9},{13,15},{18,16},{20,... | collective-permute-start | bytes 1966088 | tf_op jit(solution)/shard_map/ppermute | solution.py:196
  36.5 19.6 %collective-permute-start.4 = (f32[10,128,128]{2,1,0:T(8,128)S(1)}, f32[10,128,128]{2,1,0:T(8,128)S(1)}, u32[]{:S(2)}, u32[]{:S(2)}) collective-permute-start(f32[10,128,128]{2,1,0:T(8,128)S(1)} %collective-permute-done.3.refs_1_), channel_id=1, source_target_pairs={{2,4},{4,2},{3,5},{5,3},{10,12},{12,10},{11,13},{13,11},{18,20},{2... | collective-permute-start | bytes 1966088 | tf_op jit(solution)/shard_map/ppermute | solution.py:196
  39.6 27.4 %collective-permute-start.6 = (f32[10,128,128]{2,1,0:T(8,128)S(1)}, f32[10,128,128]{2,1,0:T(8,128)}, u32[]{:S(2)}, u32[]{:S(2)}) collective-permute-start(f32[10,128,128]{2,1,0:T(8,128)S(1)} %pad_maximum_fusion.1.refs_0_), channel_id=1, source_target_pairs={{2,4},{4,2},{3,5},{5,3},{10,12},{12,10},{11,13},{13,11},{18,20},{2... | collective-permute-start | bytes 1966088 | tf_op jit(solution)/shard_map/ppermute | solution.py:196
  43.3 28.2 %collective-permute-start.13 = (f32[9,128,256]{2,1,0:T(8,128)S(1)}, f32[9,128,256]{2,1,0:T(8,128)S(1)}, u32[]{:S(2)}, u32[]{:S(2)}) collective-permute-start(f32[9,128,256]{2,1,0:T(8,128)S(1)} %collective-permute-done.11.refs_1_), channel_id=1, source_target_pairs={{0,8},{8,0},{16,24},{24,16},{1,9},{9,1},{17,25},{25,17},{2,10},{10... | collective-permute-start | bytes 3538952 | tf_op jit(solution)/shard_map/ppermute | solution.py:196
  43.4 25.9 %collective-permute-start.7 = (f32[10,128,128]{2,1,0:T(8,128)S(1)}, f32[10,128,128]{2,1,0:T(8,128)S(1)}, u32[]{:S(2)}, u32[]{:S(2)}) collective-permute-start(f32[10,128,128]{2,1,0:T(8,128)S(1)} %collective-permute-done.2.refs_3_), channel_id=1, source_target_pairs={{2,0},{4,6},{3,1},{5,7},{10,8},{12,14},{11,9},{13,15},{18,16},{20,... | collective-permute-start | bytes 1966088 | tf_op jit(solution)/shard_map/ppermute | solution.py:196
  47.5 39.3 %collective-permute-start.12 = (f32[9,128,256]{2,1,0:T(8,128)S(1)}, f32[9,128,256]{2,1,0:T(8,128)}, u32[]{:S(2)}, u32[]{:S(2)}) collective-permute-start(f32[9,128,256]{2,1,0:T(8,128)S(1)} %copy-done), channel_id=1, source_target_pairs={{0,8},{8,0},{16,24},{24,16},{1,9},{9,1},{17,25},{25,17},{2,10},{10... | collective-permute-start | bytes 3538952 | tf_op jit(solution)/shard_map/ppermute | solution.py:196
  56.1 17.7 %collective-permute-start.14 = (f32[10,128,128]{2,1,0:T(8,128)S(1)}, f32[10,128,128]{2,1,0:T(8,128)S(1)}, u32[]{:S(2)}, u32[]{:S(2)}) collective-permute-start(f32[10,128,128]{2,1,0:T(8,128)S(1)} %collective-permute-done.4.refs_3_), channel_id=1, source_target_pairs={{2,0},{4,6},{3,1},{5,7},{10,8},{12,14},{11,9},{13,15},{18,16},{20,... | collective-permute-start | bytes 1966088 | tf_op jit(solution)/shard_map/ppermute | solution.py:196
  69.3 25.6 %collective-permute-start.10 = (f32[10,128,128]{2,1,0:T(8,128)}, f32[10,128,128]{2,1,0:T(8,128)}, u32[]{:S(2)}, u32[]{:S(2)}) collective-permute-start(f32[10,128,128]{2,1,0:T(8,128)} %collective-permute-done.6.refs_5_), channel_id=1, source_target_pairs={{2,0},{4,6},{3,1},{5,7},{10,8},{12,14},{11,9},{13,15},{18,16},{20,... | collective-permute-start | bytes 1966088 | tf_op jit(solution)/shard_map/ppermute | solution.py:196
  74.7 24.3 %collective-permute-start.15 = (f32[8,128,128]{2,1,0:T(8,128)}, f32[8,128,128]{2,1,0:T(8,128)}, u32[]{:S(2)}, u32[]{:S(2)}) collective-permute-start(f32[8,128,128]{2,1,0:T(8,128)} %pad_maximum_fusion.3.refs_0_), channel_id=1, source_target_pairs={{0,2},{2,0},{4,6},{6,4},{1,3},{3,1},{5,7},{7,5},{8,10},{10,8},{12,... | collective-permute-start | bytes 1572872 | tf_op jit(solution)/shard_map/ppermute | solution.py:196
  82.2 54.2 %collective-permute-start.22 = (f32[4,128,128]{2,1,0:T(8,128)}, f32[4,128,128]{2,1,0:T(8,128)S(1)}, u32[]{:S(2)}, u32[]{:S(2)}) collective-permute-start(f32[4,128,128]{2,1,0:T(8,128)} %get-tuple-element.104.refs_0_), channel_id=1, source_target_pairs={{2,4},{4,2},{3,5},{5,3},{10,12},{12,10},{11,13},{13,11},{18,20},{2... | collective-permute-start | bytes 786440 | tf_op jit(solution)/shard_map/ppermute | solution.py:196
  94.9 20.3 %collective-permute-start.19 = (f32[8,128,128]{2,1,0:T(8,128)}, f32[8,128,128]{2,1,0:T(8,128)S(1)}, u32[]{:S(2)}, u32[]{:S(2)}) collective-permute-start(f32[8,128,128]{2,1,0:T(8,128)} %collective-permute-done.18.refs_5_), channel_id=1, source_target_pairs={{2,0},{4,6},{3,1},{5,7},{10,8},{12,14},{11,9},{13,15},{18,16},{20,... | collective-permute-start | bytes 1572872 | tf_op jit(solution)/shard_map/ppermute | solution.py:196
  99.0 16.2 %collective-permute-start.17 = (f32[8,128,128]{2,1,0:T(8,128)}, f32[8,128,128]{2,1,0:T(8,128)S(1)}, u32[]{:S(2)}, u32[]{:S(2)}) collective-permute-start(f32[8,128,128]{2,1,0:T(8,128)} %collective-permute-done.15.refs_1_), channel_id=1, source_target_pairs={{2,4},{4,2},{3,5},{5,3},{10,12},{12,10},{11,13},{13,11},{18,20},{2... | collective-permute-start | bytes 1572872 | tf_op jit(solution)/shard_map/ppermute | solution.py:196
  101.2 16.9 %collective-permute-start.16 = (f32[4,128,128]{2,1,0:T(8,128)S(1)}, f32[4,128,128]{2,1,0:T(8,128)S(1)}, u32[]{:S(2)}, u32[]{:S(2)}) collective-permute-start(f32[4,128,128]{2,1,0:T(8,128)S(1)} %copy-done.5), channel_id=1, source_target_pairs={{0,2},{2,0},{4,6},{6,4},{1,3},{3,1},{5,7},{7,5},{8,10},{10,8},{12,... | collective-permute-start | bytes 786440 | tf_op jit(solution)/shard_map/ppermute | solution.py:196
  113.6 24.1 %collective-permute-start.20 = (f32[2,4,128,128]{3,2,1,0:T(8,128)S(1)}, f32[2,4,128,128]{3,2,1,0:T(8,128)S(1)}, u32[]{:S(2)}, u32[]{:S(2)}) collective-permute-start(f32[2,4,128,128]{3,2,1,0:T(8,128)S(1)} %get-tuple-element.95), channel_id=1, source_target_pairs={{0,1},{1,0},{2,3},{3,2},{4,5},{5,4},{6,7},{7,6},{8,9},{9,8},{10,11... | collective-permute-start | bytes 1572872 | tf_op jit(solution)/shard_map/ppermute | solution.py:196
  115.2 22.5 %collective-permute-start.21 = (f32[8,128,128]{2,1,0:T(8,128)S(1)}, f32[8,128,128]{2,1,0:T(8,128)S(1)}, u32[]{:S(2)}, u32[]{:S(2)}) collective-permute-start(f32[8,128,128]{2,1,0:T(8,128)S(1)} %collective-permute-done.17.refs_3_), channel_id=1, source_target_pairs={{2,0},{4,6},{3,1},{5,7},{10,8},{12,14},{11,9},{13,15},{18,16},{20,... | collective-permute-start | bytes 1572872 | tf_op jit(solution)/shard_map/ppermute | solution.py:196
  118.2 19.5 %collective-permute-start.24 = (f32[4,128,128]{2,1,0:T(8,128)S(1)}, f32[4,128,128]{2,1,0:T(8,128)S(1)}, u32[]{:S(2)}, u32[]{:S(2)}) collective-permute-start(f32[4,128,128]{2,1,0:T(8,128)S(1)} %collective-permute-done.16.refs_1_), channel_id=1, source_target_pairs={{2,4},{4,2},{3,5},{5,3},{10,12},{12,10},{11,13},{13,11},{18,20},{2... | collective-permute-start | bytes 786440 | tf_op jit(solution)/shard_map/ppermute | solution.py:196
  135.7 25.7 %collective-permute-start.26 = (f32[2,5,128,128]{3,2,1,0:T(8,128)S(1)}, f32[2,5,128,128]{3,2,1,0:T(8,128)S(1)}, u32[]{:S(2)}, u32[]{:S(2)}) collective-permute-start(f32[2,5,128,128]{3,2,1,0:T(8,128)S(1)} %get-tuple-element.111), channel_id=1, source_target_pairs={{0,1},{1,0},{2,3},{3,2},{4,5},{5,4},{6,7},{7,6},{8,9},{9,8},{10,11... | collective-permute-start | bytes 1966088 | tf_op jit(solution)/shard_map/ppermute | solution.py:196
  136.3 16.2 %collective-permute-start.23 = (f32[4,128,128]{2,1,0:T(8,128)S(1)}, f32[4,128,128]{2,1,0:T(8,128)S(1)}, u32[]{:S(2)}, u32[]{:S(2)}) collective-permute-start(f32[4,128,128]{2,1,0:T(8,128)S(1)} %collective-permute-done.22.refs_5_), channel_id=1, source_target_pairs={{2,0},{4,6},{3,1},{5,7},{10,8},{12,14},{11,9},{13,15},{18,16},{20,... | collective-permute-start | bytes 786440 | tf_op jit(solution)/shard_map/ppermute | solution.py:196
  150.8 14.9 %collective-permute-start.27 = (f32[2,4,128,128]{3,2,1,0:T(8,128)S(1)}, f32[2,4,128,128]{3,2,1,0:T(8,128)S(1)}, u32[]{:S(2)}, u32[]{:S(2)}) collective-permute-start(f32[2,4,128,128]{3,2,1,0:T(8,128)S(1)} %get-tuple-element.114), channel_id=1, source_target_pairs={{0,1},{1,0},{2,3},{3,2},{4,5},{5,4},{6,7},{7,6},{8,9},{9,8},{10,11... | collective-permute-start | bytes 1572872 | tf_op jit(solution)/shard_map/ppermute | solution.py:196
  (28 other events, 558.2 us)

commit v2 on v0

v2 whole, which is shorter than its diff:
```python
import functools

import jax
import jax.numpy as jnp
from jax import lax
from jax.experimental import pallas as pl
from jax.experimental.pallas import tpu as pltpu
from jax.sharding import PartitionSpec as P

VMEM_BYTES = 48 << 20
SHARES = (5, 5, 4, 2)
DEPTHS = (3, 3, 2)
FACTOR = 0.0
EFFORT = 0.0


def split(value):
    high = value.astype(jnp.bfloat16)
    low = (value - high.astype(jnp.float32)).astype(jnp.bfloat16)
    return high, low


def prepare_kernel(late, place_ref, *refs):
    outs = 4 if late else 2
    pieces, outputs = refs[:-outs], refs[-outs:]
    last = outputs[0].shape[1]
    for index, piece in enumerate(pieces):
        depth, wide = piece.shape[1:]
        half = wide // 2
        pair = split(piece[0].T)

        def store(targets, columns):
            for side in range(2):
                rows = place_ref[0] * half if side else (1 - place_ref[0]) * half
                rows = pl.ds(pl.multiple_of(rows, half), half)
                for ref, value in zip(targets, pair):
                    value = value[side * half : (side + 1) * half]
                    ref[rows, columns] = value

        if len(pieces) == 1:
            store(outputs, slice(None))
        elif not late:
            store(outputs, pl.ds(pl.multiple_of(place_ref[1 + index] * depth, depth), depth))
        else:
            column = place_ref[1 + index] * depth

            @pl.when(column < last)
            def _():
                store(outputs[:2], pl.ds(pl.multiple_of(column, depth), depth))

            @pl.when(column >= last)
            def _():
                store(outputs[2:], slice(None))


def prepare(pieces, place, late):
    channels, wide = pieces[0].shape[1:]
    depth = channels * len(pieces)
    early = depth - channels if late else depth
    shapes = [jax.ShapeDtypeStruct((3 * wide, 3 * early), jnp.bfloat16)] * 2
    blocks = [pl.BlockSpec((wide, early), lambda t, s: (t % 3, t // 3))] * 2
    if late:
        shapes += [jax.ShapeDtypeStruct((3 * wide, 3 * channels), jnp.bfloat16)] * 2
        blocks += [pl.BlockSpec((wide, channels), lambda t, s: (t % 3, t // 3))] * 2
    return pl.pallas_call(
        functools.partial(prepare_kernel, late),
        out_shape=tuple(shapes),
        grid_spec=pltpu.PrefetchScalarGridSpec(
            num_scalar_prefetch=1,
            grid=(9,),
            in_specs=[pl.BlockSpec((1,) + piece.shape[1:], lambda t, s: (t, 0, 0)) for piece in pieces],
            out_specs=tuple(blocks),
        ),
        compiler_params=pltpu.CompilerParams(vmem_limit_bytes=VMEM_BYTES),
        cost_estimate=pl.CostEstimate(flops=1000 + int(EFFORT * 1e9), bytes_accessed=1000, transcendentals=0),
    )(place, *pieces)


def conv_kernel(sources, pairs, first, last, added, place_ref, *refs):
    size = 1 + max(index for group in sources for index in group)
    arrays, refs = refs[:size], refs[size:]
    before, high_w, low_w = refs[:3]
    sums, refs = refs[3 : 3 + 2 * added], refs[3 + 2 * added :]
    results, tail, high_x, low_x = refs[:2], *refs[2:]
    channels, across = arrays[0].shape[1:]
    wide = high_w.shape[0] // 3
    half = wide // 2
    base = 1 if first else 2

    def put(side, row, slot, value):
        high, low = split(value)
        rows = pl.ds(pl.multiple_of(place_ref[slot] * channels, channels), channels)
        high_x[side, row, rows, :] = high
        low_x[side, row, rows, :] = low

    if first:
        for side in range(2):
            for slot in range(len(sources)):
                put(side, 0, slot, before[side, slot])
    else:
        for side in range(2):
            for row in range(2):
                high_x[side, row] = before[0, side, row]
                low_x[side, row] = before[1, side, row]
    for slot, group in enumerate(sources):
        for row in range(pairs):
            for side in range(2):
                from_row = 2 * pairs - 1 - row if side else row
                value = arrays[group[0]][from_row]
                for index in group[1:]:
                    value = value + arrays[index][from_row]
                put(side, base + row, slot, value)
    total = base + pairs
    for side in range(2):
        for row in range(2):
            tail[0, side, row] = high_x[side, total - 2 + row]
            tail[1, side, row] = low_x[side, total - 2 + row]
    if last:
        for side in range(2):
            high_x[side, total] = high_x[1 - side, total - 1]
            low_x[side, total] = low_x[1 - side, total - 1]
        total += 1
    outs = total - 2
    lane = lax.broadcasted_iota(jnp.int32, (wide, across), 1)
    dot = functools.partial(jnp.dot, preferred_element_type=jnp.float32)

    def step(q, carry):
        taps = [
            [jnp.concatenate([ref[0, q + a], ref[1, q + 2 - a]], axis=1) for a in range(3)] for ref in (high_x, low_x)
        ]
        high, low = taps
        rows = jnp.concatenate([high_w[...], high_w[...], low_w[...]], axis=1)
        total_sum = dot(rows, jnp.concatenate(high + low + high, axis=0))
        for side in range(2):
            lanes = slice(side * across, (side + 1) * across)
            left = pltpu.roll(total_sum[:wide, lanes], 1, 1)
            right = pltpu.roll(total_sum[2 * wide :, lanes], across - 1, 1)
            result = (
                total_sum[wide : 2 * wide, lanes]
                + jnp.where(lane == 0, 0.0, left)
                + jnp.where(lane == across - 1, 0.0, right)
            )
            row = q if side == 0 else outs - 1 - q
            for index, ref in enumerate(results):
                value = result[index * half : (index + 1) * half]
                ref[side, row] = value + sums[index][side, row] if added else value
        return carry

    lax.fori_loop(0, outs, step, 0)


def conv(place, groups, before, weights, pairs, first, last, sums=()):
    arrays, numbers = [], []
    for group in groups:
        numbers.append(tuple(range(len(arrays), len(arrays) + len(group))))
        arrays += group
    channels, across = arrays[0].shape[1:]
    depth = channels * len(groups)
    wide = weights[0].shape[0] // 3
    rows = (1 if first else 2) + pairs + (1 if last else 0)
    outs = rows - 2
    result = jax.ShapeDtypeStruct((2, outs, wide // 2, across), jnp.float32)
    tail = jax.ShapeDtypeStruct((2, 2, 2, depth, across), jnp.bfloat16)
    vmem = pl.BlockSpec(memory_space=pltpu.VMEM)
    flops = 2 * 2 * outs * across * 9 * depth * wide * 3
    return pl.pallas_call(
        functools.partial(conv_kernel, tuple(numbers), pairs, first, last, bool(sums)),
        out_shape=(result, result, tail),
        in_specs=[pl.BlockSpec(memory_space=pltpu.SMEM)] + [vmem] * (len(arrays) + 3 + len(sums)),
        out_specs=(vmem, vmem, vmem),
        scratch_shapes=[
            pltpu.VMEM((2, rows, depth, across), jnp.bfloat16),
            pltpu.VMEM((2, rows, depth, across), jnp.bfloat16),
        ],
        compiler_params=pltpu.CompilerParams(vmem_limit_bytes=VMEM_BYTES),
        cost_estimate=pl.CostEstimate(flops=1000 + int(flops * FACTOR), bytes_accessed=1000, transcendentals=0),
    )(place, *arrays, before, *weights, *sums)


class Cell:
    def __init__(self, value):
        self.value = value


def after(value, cells):
    cells = [cell for cell in cells if cell is not None]
    if not cells:
        return value
    value, *others = lax.optimization_barrier((value, *(cell.value for cell in cells)))
    for cell, other in zip(cells, others):
        cell.value = other
    return value


class Lane:
    def __init__(self, axis, most=2):
        self.axis, self.most, self.sent = axis, most, []

    def send(self, value, pairs, *cells):
        held = self.sent[-self.most] if len(self.sent) >= self.most else None
        cell = Cell(lax.ppermute(after(value, (held,) + cells), self.axis, pairs))
        self.sent.append(cell)
        return cell


def edges(count, step, parity):
    moves = []
    for low in range(parity, count - 1, 2):
        if low >= step:
            moves.append((low, low + 1))
        if low + 1 <= count - 1 - step:
            moves.append((low + 1, low))
    return moves


def gathered_keys(positions):
    keys = [0]
    bit = positions // 2
    while bit:
        keys += [key ^ bit for key in keys]
        bit //= 2
    return keys


def gathered(piece, lane):
    count = lax.axis_size("pos")
    pieces = {0: Cell(piece)}
    bit = count // 2
    while bit:
        swap = [(i, i ^ bit) for i in range(count)]
        pieces.update({key ^ bit: lane.send(cell.value, swap) for key, cell in list(pieces.items())})
        bit //= 2
    return [pieces[key] for key in gathered_keys(count)]


def chunk_sizes(half):
    total = sum(SHARES)
    return [half * share // total for share in SHARES] if half % total == 0 else [half]


ORDER = (
    ("E00",), ("O00",), ("E10",), ("O01",), ("E01",), ("O10",), ("E02",), ("O11",), ("E11",), ("O20", "X2"),
    ("P", "X3"), ("E20",), ("O21",), ("H",), ("E12", "H"), ("O30",), ("A0",), ("E21", "A0"), ("E30", "E12"), ("O31",),
    ("A1",), ("G",), ("E22", "A1"), ("B0", "A0"), ("E31",), ("A2",), ("B1",), ("E32",), ("A3",), ("B2",), ("B3",),
)


def body(activations, filters):
    count, positions = lax.axis_size("filt"), lax.axis_size("pos")
    me, position, layer = lax.axis_index("filt"), lax.axis_index("pos"), lax.axis_index("layer")
    height, channels, across = activations.shape
    half = height // 2
    forward = [(i, i + 1) for i in range(positions - 1)]
    backward = [(i + 1, i) for i, _ in forward]
    swap = [(0, 1), (1, 0)]

    sizes = chunk_sizes(half)
    starts = [sum(sizes[:i]) for i in range(len(sizes))]
    chunks = [
        jnp.concatenate([activations[s : s + m], activations[height - s - m : height - s]], axis=0)
        for s, m in zip(starts, sizes)
    ]
    lanes = {"E": Lane("filt", DEPTHS[0]), "O": Lane("filt", DEPTHS[1]), "Y": Lane("layer", DEPTHS[2])}
    by_swaps = positions & (positions - 1) == 0 and filters.shape[1] % 128 == 0
    late = by_swaps and positions == count == 4 and len(sizes) > 1
    turn = 1 - 2 * (me % 2)
    slots = jnp.arange(count)
    place = (slots if late else jnp.mod(me + turn * slots, count)).astype(jnp.int32)
    order = layer.astype(jnp.int32).reshape(1)
    if by_swaps:
        owners = jnp.stack([position ^ key for key in gathered_keys(positions)])
        owners = jnp.mod(turn * (owners - me), count) if late else owners
        order = jnp.concatenate([order, owners.astype(jnp.int32)])
    cells = {}
    first = Cell(chunks[0])
    held = after(filters, [first])
    chunks[0] = first.value
    if by_swaps:
        pieces = gathered(held, Lane("pos", 99))
    else:
        pieces = [Cell(lax.all_gather(held, "pos", axis=1, tiled=True))]
    cells.update({f"X{index}": cell for index, cell in enumerate(pieces)})

    def move(word, waits):
        kind, index, step = word[0], int(word[1]), int(word[2])
        parity = "EO".index(kind)
        source = Cell(chunks[index]) if step == 0 else cells.get("OE"[parity] + f"{index}{step - 1}")
        moves = edges(count, step, parity)
        if moves and source is not None:
            cells[word] = lanes[kind].send(source.value, moves, *waits)

    def groups(index, taken):
        result = []
        for slot in taken:
            words = [f"E{index}{slot - 1}"] + ([f"O{index}{count - 1 - slot}"] if slot >= 2 else [])
            result.append([cells[word].value for word in words if word in cells] if slot else [chunks[index]])
        return result

    def halo(taken):
        parts = groups(0, taken)
        above, below = (
            jnp.stack([sum(array[row] for array in part) for part in parts]) for row in (2 * sizes[0] - 1, 0)
        )
        return Cell(jnp.stack([lax.ppermute(above, "pos", forward), lax.ppermute(below, "pos", backward)]))

    tails, sums = {}, {}

    def compute(kind, index, waits):
        taken = {"A": range(count - 1), "B": [count - 1], "K": range(count)}[kind]
        begin, end = index == 0, index == len(chunks) - 1
        before = cells["G" if kind == "B" else "H"].value if begin else tails[kind, index - 1]
        weights = [cell.value for cell in prepared[2 * (kind == "B") :][:2]]
        extra = [cell.value for cell in sums[index]] if kind == "B" else ()
        before = after(before, waits)
        send, keep, tails[kind, index] = conv(
            place, groups(index, taken), before, weights, sizes[index], begin, end, extra
        )
        sums[index] = [Cell(send), Cell(keep)]
        cells[f"{kind}{index}"] = sums[index][1]
        if kind != "A":
            cells[f"Y{index}"] = lanes["Y"].send(send, swap)

    if late:
        plan = ORDER
    else:
        plan = [("P",)]
        for index in range(len(chunks)):
            for step in range(count - 1):
                plan += [(f"E{index}{step}",)] + ([(f"O{index}{step}",)] if step < count - 2 else [])
        plan += [("H",)] + [(f"K{index}",) for index in range(len(chunks))]
    for word, *names in plan:
        kind = word[0]
        waits = [cells[name] for name in names if name in cells]
        if kind in "EO":
            move(word, waits)
        elif kind == "P":
            arrays = [cell.value for cell in pieces]
            prepared = [Cell(array) for array in prepare(arrays, order, late)]
            cells["P"] = prepared[0]
        elif kind in "HG":
            cells[kind] = halo([count - 1] if kind == "G" else range(count - 1 if late else count))
        else:
            compute(kind, int(word[1]), waits)
    blocks = [jnp.maximum(sums[index][1].value + cells[f"Y{index}"].value, 0.0) for index in range(len(chunks))]
    return jnp.concatenate([block[0] for block in blocks] + [block[1] for block in reversed(blocks)], axis=0)


def solution(mesh):
    in_specs = (P("pos", ("layer", "filt"), None), P(None, ("layer", "pos"), "filt"))
    out_specs = P("pos", ("filt", "layer"), None)
    return jax.shard_map(body, mesh=mesh, in_specs=in_specs, out_specs=out_specs, check_vma=False)
```

time: 352 us -> 175 us (0.50)
  waiting for transfers between devices: 238 us -> 50.7 us
  matrix products: 86.7 us -> 0 us
  Pallas kernels: 0 us -> 62.3 us
  starting transfers between devices: 2.67 us -> 51.4 us
  between operations: 13.2 us -> 0.74 us
    all_gather x2 -> x0, waiting for transfers between devices: 184 us -> none  [the longest x1 148 us: body(): panel = lax.all_gather(activations, 'filt', axis=1, tiled=True)]
    dot_general x9 -> x0, matrix products: 86.7 us -> none  [convolve(): jnp.einsum('ric,io->roc', window, weights[tap_index], precision=lax.Preci...]
    pallas_call x0 -> x9, Pallas kernels: none -> 62.3 us  [the longest x8 53 us: conv(): pl.pallas_call(functools.partial(conv_kernel, tuple(numbers), pairs, firs...]
    reduce_scatter x1 -> x0, waiting for transfers between devices: 53.5 us -> none  [body(): reduced = lax.psum_scatter(summed, 'layer', scatter_dimension=1, tiled=True)]
    ppermute x2 -> x31, waiting for transfers between devices: 0.01 us -> 50.7 us  [the longest x27 49.9 us: send(): cell = Cell(lax.ppermute(after(value, (held,) + cells), self.axis, pairs))]
    ppermute x2 -> x31, starting transfers between devices: 2.59 us -> 51.4 us  [the longest x27 46.2 us: send(): cell = Cell(lax.ppermute(after(value, (held,) + cells), self.axis, pairs))]
  transfers between devices with their start and end apart: 5 -> 31, of which waited for: 3 -> 11; matrix products, arithmetic and copies ran while one was open for 6% -> 1% of each run, Pallas kernels for 0% -> 36%
where the time goes in v2:
time: 175 us; the launch traced here: 174 us
  Pallas kernels  62.3 us (36%)
  starting transfers between devices  51.4 us (29%)
  waiting for transfers between devices  50.7 us (29%)
  local copies, waits for them, and re-layouts  8.55 us (5%)
    pallas_call x8, Pallas kernels, conv(): pl.pallas_call(functools.partial(conv_kernel, tuple(numbers), pairs, firs...  53 us
    ppermute x27, waiting for transfers between devices, send(): cell = Cell(lax.ppermute(after(value, (held,) + cells), self.axis, pairs))  49.9 us
    ppermute x27, starting transfers between devices, send(): cell = Cell(lax.ppermute(after(value, (held,) + cells), self.axis, pairs))  46.2 us
    pallas_call x1, Pallas kernels, prepare(): pl.pallas_call(functools.partial(prepare_kernel, late), out_shape=tuple(s...  9.32 us
    unnamed x43, local copies, waits for them, and re-layouts  4.48 us
  transfers between devices with their start and end apart: 31, of which 11 were waited for; matrix products, arithmetic and copies ran while one was open for 1% of the time, Pallas kernels for 36%

profile of v2, /device:TPU:16, one launch (start us, length us, event | category | flops | bytes accessed | tf_op | source)
XLA Modules:
  0.0 174.4 jit_solution(16880931424271899257)
XLA Ops:
  5.3 13.9 %collective-permute-done.3.refs_1_ = f32[10,128,128]{2,1,0:T(8,128)S(1)} collective-permute-done((f32[10,128,128]{2,1,0:T(8,128)S(1)}, f32[10,128,128]{2,1,0:T(8,128)S(1)}, u32[]{:S(2)}, u32[]{:S(2)}) %collective-permute-start.3) | collective-permute-done | bytes 655392 | tf_op jit(solution)/shard_map/ppermute | solution.py:201
  19.2 2.3 %collective-permute-start.4 = (f32[10,128,128]{2,1,0:T(8,128)S(1)}, f32[10,128,128]{2,1,0:T(8,128)S(1)}, u32[]{:S(2)}, u32[]{:S(2)}) collective-permute-start(f32[10,128,128]{2,1,0:T(8,128)S(1)} %collective-permute-done.3.refs_1_), channel_id=1, source_target_pairs={{2,4},{4,2},{3,5},{5,3},{10,12},{12,10},{11,13},{13,11},{18,20},{2... | collective-permute-start | bytes 1966088 | tf_op jit(solution)/shard_map/ppermute | solution.py:201
  26.9 5.4 %collective-permute-done.refs_1_ = f32[10,128,128]{2,1,0:T(8,128)S(1)} collective-permute-done((f32[10,128,128]{2,1,0:T(8,128)S(1)}, f32[10,128,128]{2,1,0:T(8,128)S(1)}, u32[]{:S(2)}, u32[]{:S(2)}) %collective-permute-start) | collective-permute-done | bytes 655392 | tf_op jit(solution)/shard_map/ppermute | solution.py:201
  32.3 2.1 %collective-permute-start.13 = (f32[10,128,128]{2,1,0:T(8,128)S(1)}, f32[10,128,128]{2,1,0:T(8,128)}, u32[]{:S(2)}, u32[]{:S(2)}) collective-permute-start(f32[10,128,128]{2,1,0:T(8,128)S(1)} %pad_maximum_fusion.refs_0_), channel_id=1, source_target_pairs={{2,4},{4,2},{3,5},{5,3},{10,12},{12,10},{11,13},{13,11},{18,20},{2... | collective-permute-start | bytes 1966088 | tf_op jit(solution)/shard_map/ppermute | solution.py:201
  35.5 2.7 %collective-permute-start.2 = (f32[10,128,128]{2,1,0:T(8,128)S(1)}, f32[10,128,128]{2,1,0:T(8,128)}, u32[]{:S(2)}, u32[]{:S(2)}) collective-permute-start(f32[10,128,128]{2,1,0:T(8,128)S(1)} %collective-permute-done.refs_1_), channel_id=1, source_target_pairs={{2,4},{4,2},{3,5},{5,3},{10,12},{12,10},{11,13},{13,11},{18,20},{2... | collective-permute-start | bytes 1966088 | tf_op jit(solution)/shard_map/ppermute | solution.py:201
  40.6 5.7 %collective-permute-done.6.refs_2_ = f32[10,128,128]{2,1,0:T(8,128)S(1)} collective-permute-done((f32[10,128,128]{2,1,0:T(8,128)S(1)}, f32[10,128,128]{2,1,0:T(8,128)S(1)}, u32[]{:S(2)}, u32[]{:S(2)}) %collective-permute-start.6) | collective-permute-done | bytes 655392 | tf_op jit(solution)/shard_map/ppermute | solution.py:201
  49.3 2.7 %collective-permute-done.13.refs_1_ = f32[10,128,128]{2,1,0:T(8,128)} collective-permute-done((f32[10,128,128]{2,1,0:T(8,128)S(1)}, f32[10,128,128]{2,1,0:T(8,128)}, u32[]{:S(2)}, u32[]{:S(2)}) %collective-permute-start.13) | collective-permute-done | bytes 655392 | tf_op jit(solution)/shard_map/ppermute | solution.py:201
  54.3 3.8 %collective-permute-start.14 = (f32[10,128,128]{2,1,0:T(8,128)}, f32[10,128,128]{2,1,0:T(8,128)}, u32[]{:S(2)}, u32[]{:S(2)}) collective-permute-start(f32[10,128,128]{2,1,0:T(8,128)} %collective-permute-done.13.refs_1_), channel_id=1, source_target_pairs={{2,0},{4,6},{3,1},{5,7},{10,8},{12,14},{11,9},{13,15},{18,16},{20,... | collective-permute-start | bytes 1966088 | tf_op jit(solution)/shard_map/ppermute | solution.py:201
  58.2 5.7 %collective-permute-done.2.refs_3_ = f32[10,128,128]{2,1,0:T(8,128)} collective-permute-done((f32[10,128,128]{2,1,0:T(8,128)S(1)}, f32[10,128,128]{2,1,0:T(8,128)}, u32[]{:S(2)}, u32[]{:S(2)}) %collective-permute-start.2) | collective-permute-done | bytes 655392 | tf_op jit(solution)/shard_map/ppermute | solution.py:201
  63.8 2.2 %collective-permute-start.19 = (f32[10,128,128]{2,1,0:T(8,128)}, f32[10,128,128]{2,1,0:T(8,128)}, u32[]{:S(2)}, u32[]{:S(2)}) collective-permute-start(f32[10,128,128]{2,1,0:T(8,128)} %collective-permute-done.2.refs_3_), channel_id=1, source_target_pairs={{2,0},{4,6},{3,1},{5,7},{10,8},{12,14},{11,9},{13,15},{18,16},{20,... | collective-permute-start | bytes 1966088 | tf_op jit(solution)/shard_map/ppermute | solution.py:201
  68.2 3.5 %collective-permute-done.17.refs_1_ = f32[8,128,128]{2,1,0:T(8,128)} collective-permute-done((f32[8,128,128]{2,1,0:T(8,128)S(1)}, f32[8,128,128]{2,1,0:T(8,128)}, u32[]{:S(2)}, u32[]{:S(2)}) %collective-permute-start.17) | collective-permute-done | bytes 524320 | tf_op jit(solution)/shard_map/ppermute | solution.py:201
  74.9 3.9 %collective-permute-start.18 = (f32[8,128,128]{2,1,0:T(8,128)}, f32[8,128,128]{2,1,0:T(8,128)}, u32[]{:S(2)}, u32[]{:S(2)}) collective-permute-start(f32[8,128,128]{2,1,0:T(8,128)} %collective-permute-done.17.refs_1_), channel_id=1, source_target_pairs={{2,4},{4,2},{3,5},{5,3},{10,12},{12,10},{11,13},{13,11},{18,20},{2... | collective-permute-start | bytes 1572872 | tf_op jit(solution)/shard_map/ppermute | solution.py:201
  80.3 9.3 %shard_map.28 = (bf16[768,1152]{1,0:T(8,128)(2,1)}, bf16[768,1152]{1,0:T(8,128)(2,1)}, bf16[768,384]{1,0:T(8,128)(2,1)S(1)}, bf16[768,384]{1,0:T(8,128)(2,1)S(1)}) custom-call(s32[5]{0:T(128)S(1)} %pad_add_fusion.place_ref, f32[9,128,256]{2,1,0:T(8,128)S(1)} %copy-done.1, f32[9,128,256]{2,1,0:T(8,128)} %collective-permute-done.15.refs_1_, ...), custom_call_target="tpu_custom_call" | custom-call | flops 1000 | bytes 1000 | tf_op jit(solution)/shard_map/pallas_call | solution.py:65
  89.7 9.0 %shard_map.29 = (f32[2,4,128,128]{3,2,1,0:T(8,128)S(1)}, f32[2,4,128,128]{3,2,1,0:T(8,128)S(1)}, bf16[2,2,2,384,128]{4,3,2,1,0:T(8,128)(2,1)S(1)}) custom-call(s32[4]{0:T(128)S(1)} %iota.18.place_ref, f32[10,128,128]{2,1,0:T(8,128)S(1)} %pad_maximum_fusion.1.refs_0_, f32[10,128,128]{2,1,0:T(8,128)S(1)} %copy-done.8, f32[10,128,128]{2,1,0:T(8,128)S(1)} %copy-done.14, ...), custom_call_target="tpu_custom_call" | custom-call | flops 1000 | bytes 1000 | tf_op jit(solution)/shard_map/pallas_call | solution.py:166
  100.4 11.1 %shard_map.31 = (f32[2,5,128,128]{3,2,1,0:T(8,128)S(1)}, f32[2,5,128,128]{3,2,1,0:T(8,128)S(1)}, bf16[2,2,2,384,128]{4,3,2,1,0:T(8,128)(2,1)S(1)}) custom-call(s32[4]{0:T(128)S(1)} %iota.20.place_ref, f32[10,128,128]{2,1,0:T(8,128)S(1)} %pad_maximum_fusion.refs_0_, f32[10,128,128]{2,1,0:T(8,128)S(1)} %copy-done.16, ...), custom_call_target="tpu_custom_call" | custom-call | flops 1000 | bytes 1000 | tf_op jit(solution)/shard_map/pallas_call | solution.py:166
  111.7 3.9 %collective-permute-start.20 = (f32[8,128,128]{2,1,0:T(8,128)}, f32[8,128,128]{2,1,0:T(8,128)S(1)}, u32[]{:S(2)}, u32[]{:S(2)}) collective-permute-start(f32[8,128,128]{2,1,0:T(8,128)} %collective-permute-done.18.refs_3_), channel_id=1, source_target_pairs={{2,0},{4,6},{3,1},{5,7},{10,8},{12,14},{11,9},{13,15},{18,16},{20,... | collective-permute-start | bytes 1572872 | tf_op jit(solution)/shard_map/ppermute | solution.py:201
  115.6 3.7 %shard_map.30 = (f32[2,4,128,128]{3,2,1,0:T(8,128)S(1)}, f32[2,4,128,128]{3,2,1,0:T(8,128)S(1)}, bf16[2,2,2,128,128]{4,3,2,1,0:T(8,128)(2,1)S(1)}) custom-call(s32[4]{0:T(128)S(1)} %iota.17.place_ref, f32[10,128,128]{2,1,0:T(8,128)S(1)} %copy-done.10, f32[10,128,128]{2,1,0:T(8,128)S(1)} %copy-done.6, f32[2,1,128,128]{3,2,1,0:T(8,128)S(1)} %pad_maximum_fusion.6.refs_2_, ...), custom_call_target="tpu_custom_call" | custom-call | flops 1000 | bytes 1000 | tf_op jit(solution)/shard_map/pallas_call | solution.py:166
  122.9 3.9 %collective-permute-start.25 = (f32[4,128,128]{2,1,0:T(8,128)S(1)}, f32[4,128,128]{2,1,0:T(8,128)S(1)}, u32[]{:S(2)}, u32[]{:S(2)}) collective-permute-start(f32[4,128,128]{2,1,0:T(8,128)S(1)} %collective-permute-done.21.refs_1_), channel_id=1, source_target_pairs={{2,4},{4,2},{3,5},{5,3},{10,12},{12,10},{11,13},{13,11},{18,20},{2... | collective-permute-start | bytes 786440 | tf_op jit(solution)/shard_map/ppermute | solution.py:201
  126.8 5.2 %shard_map.32 = (f32[2,5,128,128]{3,2,1,0:T(8,128)S(1)}, f32[2,5,128,128]{3,2,1,0:T(8,128)S(1)}, bf16[2,2,2,128,128]{4,3,2,1,0:T(8,128)(2,1)S(1)}) custom-call(s32[4]{0:T(128)S(1)} %iota.21.place_ref, f32[10,128,128]{2,1,0:T(8,128)} %collective-permute-done.19.refs_0_, f32[10,128,128]{2,1,0:T(8,128)} %collective-permute-done.13.refs_1_, ...), custom_call_target="tpu_custom_call" | custom-call | flops 1000 | bytes 1000 | tf_op jit(solution)/shard_map/pallas_call | solution.py:166
  133.9 9.3 %shard_map.33 = (f32[2,4,128,128]{3,2,1,0:T(8,128)S(1)}, f32[2,4,128,128]{3,2,1,0:T(8,128)S(1)}, bf16[2,2,2,384,128]{4,3,2,1,0:T(8,128)(2,1)S(1)}) custom-call(s32[4]{0:T(128)S(1)} %iota.22.place_ref, f32[8,128,128]{2,1,0:T(8,128)S(1)} %pad_maximum_fusion.2.refs_0_, f32[8,128,128]{2,1,0:T(8,128)} %collective-permute-done.17.refs_1_, ...), custom_call_target="tpu_custom_call" | custom-call | flops 1000 | bytes 1000 | tf_op jit(solution)/shard_map/pallas_call | solution.py:166
  144.7 4.3 %shard_map.34 = (f32[2,4,128,128]{3,2,1,0:T(8,128)S(1)}, f32[2,4,128,128]{3,2,1,0:T(8,128)S(1)}, bf16[2,2,2,128,128]{4,3,2,1,0:T(8,128)(2,1)S(1)}) custom-call(s32[4]{0:T(128)S(1)} %iota.19.place_ref, f32[8,128,128]{2,1,0:T(8,128)S(1)} %collective-permute-done.20.refs_0_, f32[8,128,128]{2,1,0:T(8,128)} %collective-permute-done.12.refs_1_, ...), custom_call_target="tpu_custom_call" | custom-call | flops 1000 | bytes 1000 | tf_op jit(solution)/shard_map/pallas_call | solution.py:166
  150.8 6.7 %shard_map.35 = (f32[2,3,128,128]{3,2,1,0:T(8,128)S(1)}, f32[2,3,128,128]{3,2,1,0:T(8,128)S(1)}, bf16[2,2,2,384,128]{4,3,2,1,0:T(8,128)(2,1)}) custom-call(s32[4]{0:T(128)S(1)} %iota.24.place_ref, f32[4,128,128]{2,1,0:T(8,128)S(1)} %copy-done.4, f32[4,128,128]{2,1,0:T(8,128)S(1)} %collective-permute-done.21.refs_1_, ...), custom_call_target="tpu_custom_call" | custom-call | flops 1000 | bytes 1000 | tf_op jit(solution)/shard_map/pallas_call | solution.py:166
  157.6 3.6 %shard_map.36 = (f32[2,3,128,128]{3,2,1,0:T(8,128)S(1)}, f32[2,3,128,128]{3,2,1,0:T(8,128)S(1)}, bf16[2,2,2,128,128]{4,3,2,1,0:T(8,128)(2,1)}) custom-call(s32[4]{0:T(128)S(1)} %iota.23.place_ref, f32[4,128,128]{2,1,0:T(8,128)S(1)} %collective-permute-done.26.refs_0_, f32[4,128,128]{2,1,0:T(8,128)S(1)} %collective-permute-done.22.refs_1_, ...), custom_call_target="tpu_custom_call" | custom-call | flops 1000 | bytes 1000 | tf_op jit(solution)/shard_map/pallas_call | solution.py:166
  163.4 8.8 %collective-permute-done.30 = f32[2,3,128,128]{3,2,1,0:T(8,128)S(1)} collective-permute-done((f32[2,3,128,128]{3,2,1,0:T(8,128)S(1)}, f32[2,3,128,128]{3,2,1,0:T(8,128)S(1)}, u32[]{:S(2)}, u32[]{:S(2)}) %collective-permute-start.30) | collective-permute-done | bytes 393248 | tf_op jit(solution)/shard_map/ppermute | solution.py:201
  (118 shorter events, 40.7 us)
Async XLA Ops:
  1.5 17.7 %collective-permute-start.3 = (f32[10,128,128]{2,1,0:T(8,128)S(1)}, f32[10,128,128]{2,1,0:T(8,128)S(1)}, u32[]{:S(2)}, u32[]{:S(2)}) collective-permute-start(f32[10,128,128]{2,1,0:T(8,128)S(1)} %pad_maximum_fusion.1.refs_0_), channel_id=1, source_target_pairs={{0,2},{2,0},{4,6},{6,4},{1,3},{3,1},{5,7},{7,5},{8,10},{10,8},{12,... | collective-permute-start | bytes 1966088 | tf_op jit(solution)/shard_map/ppermute | solution.py:201
  3.2 18.4 %collective-permute-start.1 = (f32[10,128,128]{2,1,0:T(8,128)S(1)}, f32[10,128,128]{2,1,0:T(8,128)S(1)}, u32[]{:S(2)}, u32[]{:S(2)}) collective-permute-start(f32[10,128,128]{2,1,0:T(8,128)S(1)} %pad_maximum_fusion.1.refs_0_), channel_id=1, source_target_pairs={{2,4},{4,2},{3,5},{5,3},{10,12},{12,10},{11,13},{13,11},{18,20},{2... | collective-permute-start | bytes 1966088 | tf_op jit(solution)/shard_map/ppermute | solution.py:201
  5.1 34.0 %collective-permute-start.7 = (f32[9,128,256]{2,1,0:T(8,128)S(1)}, f32[9,128,256]{2,1,0:T(8,128)S(1)}, u32[]{:S(2)}, u32[]{:S(2)}) collective-permute-start(f32[9,128,256]{2,1,0:T(8,128)S(1)} %copy-done.1), channel_id=1, source_target_pairs={{0,8},{8,0},{16,24},{24,16},{1,9},{9,1},{17,25},{25,17},{2,10},{10... | collective-permute-start | bytes 3538952 | tf_op jit(solution)/shard_map/ppermute | solution.py:201
  5.2 27.1 %collective-permute-start = (f32[10,128,128]{2,1,0:T(8,128)S(1)}, f32[10,128,128]{2,1,0:T(8,128)S(1)}, u32[]{:S(2)}, u32[]{:S(2)}) collective-permute-start(f32[10,128,128]{2,1,0:T(8,128)S(1)} %pad_maximum_fusion.refs_0_), channel_id=1, source_target_pairs={{0,2},{2,0},{4,6},{6,4},{1,3},{3,1},{5,7},{7,5},{8,10},{10,8},{12,... | collective-permute-start | bytes 1966088 | tf_op jit(solution)/shard_map/ppermute | solution.py:201
  19.2 16.3 %collective-permute-start.4 = (f32[10,128,128]{2,1,0:T(8,128)S(1)}, f32[10,128,128]{2,1,0:T(8,128)S(1)}, u32[]{:S(2)}, u32[]{:S(2)}) collective-permute-start(f32[10,128,128]{2,1,0:T(8,128)S(1)} %collective-permute-done.3.refs_1_), channel_id=1, source_target_pairs={{2,4},{4,2},{3,5},{5,3},{10,12},{12,10},{11,13},{13,11},{18,20},{2... | collective-permute-start | bytes 1966088 | tf_op jit(solution)/shard_map/ppermute | solution.py:201
  21.6 24.8 %collective-permute-start.6 = (f32[10,128,128]{2,1,0:T(8,128)S(1)}, f32[10,128,128]{2,1,0:T(8,128)S(1)}, u32[]{:S(2)}, u32[]{:S(2)}) collective-permute-start(f32[10,128,128]{2,1,0:T(8,128)S(1)} %collective-permute-done.1.refs_1_), channel_id=1, source_target_pairs={{2,0},{4,6},{3,1},{5,7},{10,8},{12,14},{11,9},{13,15},{18,16},{20,... | collective-permute-start | bytes 1966088 | tf_op jit(solution)/shard_map/ppermute | solution.py:201
  23.5 25.8 %collective-permute-start.15 = (f32[9,128,256]{2,1,0:T(8,128)S(1)}, f32[9,128,256]{2,1,0:T(8,128)}, u32[]{:S(2)}, u32[]{:S(2)}) collective-permute-start(f32[9,128,256]{2,1,0:T(8,128)S(1)} %copy-done.1), channel_id=1, source_target_pairs={{0,16},{8,24},{16,0},{24,8},{1,17},{9,25},{17,1},{25,9},{2,18},{10... | collective-permute-start | bytes 3538952 | tf_op jit(solution)/shard_map/ppermute | solution.py:201
  32.3 19.7 %collective-permute-start.13 = (f32[10,128,128]{2,1,0:T(8,128)S(1)}, f32[10,128,128]{2,1,0:T(8,128)}, u32[]{:S(2)}, u32[]{:S(2)}) collective-permute-start(f32[10,128,128]{2,1,0:T(8,128)S(1)} %pad_maximum_fusion.refs_0_), channel_id=1, source_target_pairs={{2,4},{4,2},{3,5},{5,3},{10,12},{12,10},{11,13},{13,11},{18,20},{2... | collective-permute-start | bytes 1966088 | tf_op jit(solution)/shard_map/ppermute | solution.py:201
  35.5 28.3 %collective-permute-start.2 = (f32[10,128,128]{2,1,0:T(8,128)S(1)}, f32[10,128,128]{2,1,0:T(8,128)}, u32[]{:S(2)}, u32[]{:S(2)}) collective-permute-start(f32[10,128,128]{2,1,0:T(8,128)S(1)} %collective-permute-done.refs_1_), channel_id=1, source_target_pairs={{2,4},{4,2},{3,5},{5,3},{10,12},{12,10},{11,13},{13,11},{18,20},{2... | collective-permute-start | bytes 1966088 | tf_op jit(solution)/shard_map/ppermute | solution.py:201
  39.1 24.8 %collective-permute-start.5 = (f32[10,128,128]{2,1,0:T(8,128)S(1)}, f32[10,128,128]{2,1,0:T(8,128)S(1)}, u32[]{:S(2)}, u32[]{:S(2)}) collective-permute-start(f32[10,128,128]{2,1,0:T(8,128)S(1)} %collective-permute-done.4.refs_3_), channel_id=1, source_target_pairs={{2,0},{4,6},{3,1},{5,7},{10,8},{12,14},{11,9},{13,15},{18,16},{20,... | collective-permute-start | bytes 1966088 | tf_op jit(solution)/shard_map/ppermute | solution.py:201
  49.2 29.8 %collective-permute-start.16 = (f32[9,128,256]{2,1,0:T(8,128)}, f32[9,128,256]{2,1,0:T(8,128)}, u32[]{:S(2)}, u32[]{:S(2)}) collective-permute-start(f32[9,128,256]{2,1,0:T(8,128)} %collective-permute-done.15.refs_1_), channel_id=1, source_target_pairs={{0,8},{8,0},{16,24},{24,16},{1,9},{9,1},{17,25},{25,17},{2,10},{10... | collective-permute-start | bytes 3538952 | tf_op jit(solution)/shard_map/ppermute | solution.py:201
  53.3 18.4 %collective-permute-start.17 = (f32[8,128,128]{2,1,0:T(8,128)S(1)}, f32[8,128,128]{2,1,0:T(8,128)}, u32[]{:S(2)}, u32[]{:S(2)}) collective-permute-start(f32[8,128,128]{2,1,0:T(8,128)S(1)} %pad_maximum_fusion.2.refs_0_), channel_id=1, source_target_pairs={{0,2},{2,0},{4,6},{6,4},{1,3},{3,1},{5,7},{7,5},{8,10},{10,8},{12,... | collective-permute-start | bytes 1572872 | tf_op jit(solution)/shard_map/ppermute | solution.py:201
  54.3 44.4 %collective-permute-start.14 = (f32[10,128,128]{2,1,0:T(8,128)}, f32[10,128,128]{2,1,0:T(8,128)}, u32[]{:S(2)}, u32[]{:S(2)}) collective-permute-start(f32[10,128,128]{2,1,0:T(8,128)} %collective-permute-done.13.refs_1_), channel_id=1, source_target_pairs={{2,0},{4,6},{3,1},{5,7},{10,8},{12,14},{11,9},{13,15},{18,16},{20,... | collective-permute-start | bytes 1966088 | tf_op jit(solution)/shard_map/ppermute | solution.py:201
  63.8 47.7 %collective-permute-start.19 = (f32[10,128,128]{2,1,0:T(8,128)}, f32[10,128,128]{2,1,0:T(8,128)}, u32[]{:S(2)}, u32[]{:S(2)}) collective-permute-start(f32[10,128,128]{2,1,0:T(8,128)} %collective-permute-done.2.refs_3_), channel_id=1, source_target_pairs={{2,0},{4,6},{3,1},{5,7},{10,8},{12,14},{11,9},{13,15},{18,16},{20,... | collective-permute-start | bytes 1966088 | tf_op jit(solution)/shard_map/ppermute | solution.py:201
  73.0 25.8 %collective-permute-start.12 = (f32[8,128,128]{2,1,0:T(8,128)S(1)}, f32[8,128,128]{2,1,0:T(8,128)}, u32[]{:S(2)}, u32[]{:S(2)}) collective-permute-start(f32[8,128,128]{2,1,0:T(8,128)S(1)} %pad_maximum_fusion.2.refs_0_), channel_id=1, source_target_pairs={{2,4},{4,2},{3,5},{5,3},{10,12},{12,10},{11,13},{13,11},{18,20},{2... | collective-permute-start | bytes 1572872 | tf_op jit(solution)/shard_map/ppermute | solution.py:201
  74.9 36.7 %collective-permute-start.18 = (f32[8,128,128]{2,1,0:T(8,128)}, f32[8,128,128]{2,1,0:T(8,128)}, u32[]{:S(2)}, u32[]{:S(2)}) collective-permute-start(f32[8,128,128]{2,1,0:T(8,128)} %collective-permute-done.17.refs_1_), channel_id=1, source_target_pairs={{2,4},{4,2},{3,5},{5,3},{10,12},{12,10},{11,13},{13,11},{18,20},{2... | collective-permute-start | bytes 1572872 | tf_op jit(solution)/shard_map/ppermute | solution.py:201
  98.8 33.8 %collective-permute-start.23 = (f32[8,128,128]{2,1,0:T(8,128)}, f32[8,128,128]{2,1,0:T(8,128)S(1)}, u32[]{:S(2)}, u32[]{:S(2)}) collective-permute-start(f32[8,128,128]{2,1,0:T(8,128)} %collective-permute-done.12.refs_1_), channel_id=1, source_target_pairs={{2,0},{4,6},{3,1},{5,7},{10,8},{12,14},{11,9},{13,15},{18,16},{20,... | collective-permute-start | bytes 1572872 | tf_op jit(solution)/shard_map/ppermute | solution.py:201
  111.7 33.0 %collective-permute-start.20 = (f32[8,128,128]{2,1,0:T(8,128)}, f32[8,128,128]{2,1,0:T(8,128)S(1)}, u32[]{:S(2)}, u32[]{:S(2)}) collective-permute-start(f32[8,128,128]{2,1,0:T(8,128)} %collective-permute-done.18.refs_3_), channel_id=1, source_target_pairs={{2,0},{4,6},{3,1},{5,7},{10,8},{12,14},{11,9},{13,15},{18,16},{20,... | collective-permute-start | bytes 1572872 | tf_op jit(solution)/shard_map/ppermute | solution.py:201
  119.3 29.7 %collective-permute-start.24 = (f32[2,4,128,128]{3,2,1,0:T(8,128)S(1)}, f32[2,4,128,128]{3,2,1,0:T(8,128)S(1)}, u32[]{:S(2)}, u32[]{:S(2)}) collective-permute-start(f32[2,4,128,128]{3,2,1,0:T(8,128)S(1)} %get-tuple-element.119), channel_id=1, source_target_pairs={{0,1},{1,0},{2,3},{3,2},{4,5},{5,4},{6,7},{7,6},{8,9},{9,8},{10,11... | collective-permute-start | bytes 1572872 | tf_op jit(solution)/shard_map/ppermute | solution.py:201
  122.9 20.3 %collective-permute-start.25 = (f32[4,128,128]{2,1,0:T(8,128)S(1)}, f32[4,128,128]{2,1,0:T(8,128)S(1)}, u32[]{:S(2)}, u32[]{:S(2)}) collective-permute-start(f32[4,128,128]{2,1,0:T(8,128)S(1)} %collective-permute-done.21.refs_1_), channel_id=1, source_target_pairs={{2,4},{4,2},{3,5},{5,3},{10,12},{12,10},{11,13},{13,11},{18,20},{2... | collective-permute-start | bytes 786440 | tf_op jit(solution)/shard_map/ppermute | solution.py:201
  132.0 29.1 %collective-permute-start.28 = (f32[2,5,128,128]{3,2,1,0:T(8,128)S(1)}, f32[2,5,128,128]{3,2,1,0:T(8,128)S(1)}, u32[]{:S(2)}, u32[]{:S(2)}) collective-permute-start(f32[2,5,128,128]{3,2,1,0:T(8,128)S(1)} %get-tuple-element.131), channel_id=1, source_target_pairs={{0,1},{1,0},{2,3},{3,2},{4,5},{5,4},{6,7},{7,6},{8,9},{9,8},{10,11... | collective-permute-start | bytes 1966088 | tf_op jit(solution)/shard_map/ppermute | solution.py:201
  132.6 18.2 %collective-permute-start.27 = (f32[4,128,128]{2,1,0:T(8,128)S(1)}, f32[4,128,128]{2,1,0:T(8,128)S(1)}, u32[]{:S(2)}, u32[]{:S(2)}) collective-permute-start(f32[4,128,128]{2,1,0:T(8,128)S(1)} %collective-permute-done.22.refs_1_), channel_id=1, source_target_pairs={{2,0},{4,6},{3,1},{5,7},{10,8},{12,14},{11,9},{13,15},{18,16},{20,... | collective-permute-start | bytes 786440 | tf_op jit(solution)/shard_map/ppermute | solution.py:201
  143.2 14.3 %collective-permute-start.26 = (f32[4,128,128]{2,1,0:T(8,128)S(1)}, f32[4,128,128]{2,1,0:T(8,128)S(1)}, u32[]{:S(2)}, u32[]{:S(2)}) collective-permute-start(f32[4,128,128]{2,1,0:T(8,128)S(1)} %collective-permute-done.25.refs_3_), channel_id=1, source_target_pairs={{2,0},{4,6},{3,1},{5,7},{10,8},{12,14},{11,9},{13,15},{18,16},{20,... | collective-permute-start | bytes 786440 | tf_op jit(solution)/shard_map/ppermute | solution.py:201
  149.1 14.2 %collective-permute-start.29 = (f32[2,4,128,128]{3,2,1,0:T(8,128)S(1)}, f32[2,4,128,128]{3,2,1,0:T(8,128)S(1)}, u32[]{:S(2)}, u32[]{:S(2)}) collective-permute-start(f32[2,4,128,128]{3,2,1,0:T(8,128)S(1)} %get-tuple-element.134), channel_id=1, source_target_pairs={{0,1},{1,0},{2,3},{3,2},{4,5},{5,4},{6,7},{7,6},{8,9},{9,8},{10,11... | collective-permute-start | bytes 1572872 | tf_op jit(solution)/shard_map/ppermute | solution.py:201
  (25 other events, 322.1 us)

commit v3 on v2

--- a/solution.py
+++ b/solution.py
@@ -27,7 +27,7 @@
     for index, piece in enumerate(pieces):
         depth, wide = piece.shape[1:]
         half = wide // 2
-        pair = split(piece[0].T)
+        pair = [value.T for value in split(piece[0])]
 
         def store(targets, columns):
             for side in range(2):

time: 175 us -> 175 us (level)
  no operation moved by 1% of the time
where the time goes in v3:
time: 175 us; the launch traced here: 174 us
  Pallas kernels  61.9 us (35%)
  starting transfers between devices  51.4 us (29%)
  waiting for transfers between devices  50.7 us (29%)
  local copies, waits for them, and re-layouts  8.55 us (5%)
    pallas_call x8, Pallas kernels, conv(): pl.pallas_call(functools.partial(conv_kernel, tuple(numbers), pairs, firs...  53 us
    ppermute x27, waiting for transfers between devices, send(): cell = Cell(lax.ppermute(after(value, (held,) + cells), self.axis, pairs))  49.9 us
    ppermute x27, starting transfers between devices, send(): cell = Cell(lax.ppermute(after(value, (held,) + cells), self.axis, pairs))  46.2 us
    pallas_call x1, Pallas kernels, prepare(): pl.pallas_call(functools.partial(prepare_kernel, late), out_shape=tuple(s...  8.9 us
    unnamed x43, local copies, waits for them, and re-layouts  4.48 us
  transfers between devices with their start and end apart: 31, of which 11 were waited for; matrix products, arithmetic and copies ran while one was open for 1% of the time, Pallas kernels for 36%

profile of v3, /device:TPU:16, one launch (start us, length us, event | category | flops | bytes accessed | tf_op | source)
XLA Modules:
  0.0 173.9 jit_solution(543917598240883464)
XLA Ops:
  5.3 13.9 %collective-permute-done.3.refs_1_ = f32[10,128,128]{2,1,0:T(8,128)S(1)} collective-permute-done((f32[10,128,128]{2,1,0:T(8,128)S(1)}, f32[10,128,128]{2,1,0:T(8,128)S(1)}, u32[]{:S(2)}, u32[]{:S(2)}) %collective-permute-start.3) | collective-permute-done | bytes 655392 | tf_op jit(solution)/shard_map/ppermute | solution.py:201
  19.2 2.3 %collective-permute-start.4 = (f32[10,128,128]{2,1,0:T(8,128)S(1)}, f32[10,128,128]{2,1,0:T(8,128)S(1)}, u32[]{:S(2)}, u32[]{:S(2)}) collective-permute-start(f32[10,128,128]{2,1,0:T(8,128)S(1)} %collective-permute-done.3.refs_1_), channel_id=1, source_target_pairs={{2,4},{4,2},{3,5},{5,3},{10,12},{12,10},{11,13},{13,11},{18,20},{2... | collective-permute-start | bytes 1966088 | tf_op jit(solution)/shard_map/ppermute | solution.py:201
  26.9 5.4 %collective-permute-done.refs_1_ = f32[10,128,128]{2,1,0:T(8,128)S(1)} collective-permute-done((f32[10,128,128]{2,1,0:T(8,128)S(1)}, f32[10,128,128]{2,1,0:T(8,128)S(1)}, u32[]{:S(2)}, u32[]{:S(2)}) %collective-permute-start) | collective-permute-done | bytes 655392 | tf_op jit(solution)/shard_map/ppermute | solution.py:201
  32.3 2.1 %collective-permute-start.13 = (f32[10,128,128]{2,1,0:T(8,128)S(1)}, f32[10,128,128]{2,1,0:T(8,128)}, u32[]{:S(2)}, u32[]{:S(2)}) collective-permute-start(f32[10,128,128]{2,1,0:T(8,128)S(1)} %pad_maximum_fusion.refs_0_), channel_id=1, source_target_pairs={{2,4},{4,2},{3,5},{5,3},{10,12},{12,10},{11,13},{13,11},{18,20},{2... | collective-permute-start | bytes 1966088 | tf_op jit(solution)/shard_map/ppermute | solution.py:201
  35.5 2.7 %collective-permute-start.2 = (f32[10,128,128]{2,1,0:T(8,128)S(1)}, f32[10,128,128]{2,1,0:T(8,128)}, u32[]{:S(2)}, u32[]{:S(2)}) collective-permute-start(f32[10,128,128]{2,1,0:T(8,128)S(1)} %collective-permute-done.refs_1_), channel_id=1, source_target_pairs={{2,4},{4,2},{3,5},{5,3},{10,12},{12,10},{11,13},{13,11},{18,20},{2... | collective-permute-start | bytes 1966088 | tf_op jit(solution)/shard_map/ppermute | solution.py:201
  40.6 5.7 %collective-permute-done.6.refs_2_ = f32[10,128,128]{2,1,0:T(8,128)S(1)} collective-permute-done((f32[10,128,128]{2,1,0:T(8,128)S(1)}, f32[10,128,128]{2,1,0:T(8,128)S(1)}, u32[]{:S(2)}, u32[]{:S(2)}) %collective-permute-start.6) | collective-permute-done | bytes 655392 | tf_op jit(solution)/shard_map/ppermute | solution.py:201
  49.3 2.7 %collective-permute-done.13.refs_1_ = f32[10,128,128]{2,1,0:T(8,128)} collective-permute-done((f32[10,128,128]{2,1,0:T(8,128)S(1)}, f32[10,128,128]{2,1,0:T(8,128)}, u32[]{:S(2)}, u32[]{:S(2)}) %collective-permute-start.13) | collective-permute-done | bytes 655392 | tf_op jit(solution)/shard_map/ppermute | solution.py:201
  54.3 3.8 %collective-permute-start.14 = (f32[10,128,128]{2,1,0:T(8,128)}, f32[10,128,128]{2,1,0:T(8,128)}, u32[]{:S(2)}, u32[]{:S(2)}) collective-permute-start(f32[10,128,128]{2,1,0:T(8,128)} %collective-permute-done.13.refs_1_), channel_id=1, source_target_pairs={{2,0},{4,6},{3,1},{5,7},{10,8},{12,14},{11,9},{13,15},{18,16},{20,... | collective-permute-start | bytes 1966088 | tf_op jit(solution)/shard_map/ppermute | solution.py:201
  58.2 5.7 %collective-permute-done.2.refs_3_ = f32[10,128,128]{2,1,0:T(8,128)} collective-permute-done((f32[10,128,128]{2,1,0:T(8,128)S(1)}, f32[10,128,128]{2,1,0:T(8,128)}, u32[]{:S(2)}, u32[]{:S(2)}) %collective-permute-start.2) | collective-permute-done | bytes 655392 | tf_op jit(solution)/shard_map/ppermute | solution.py:201
  63.8 2.2 %collective-permute-start.19 = (f32[10,128,128]{2,1,0:T(8,128)}, f32[10,128,128]{2,1,0:T(8,128)}, u32[]{:S(2)}, u32[]{:S(2)}) collective-permute-start(f32[10,128,128]{2,1,0:T(8,128)} %collective-permute-done.2.refs_3_), channel_id=1, source_target_pairs={{2,0},{4,6},{3,1},{5,7},{10,8},{12,14},{11,9},{13,15},{18,16},{20,... | collective-permute-start | bytes 1966088 | tf_op jit(solution)/shard_map/ppermute | solution.py:201
  68.2 3.5 %collective-permute-done.17.refs_1_ = f32[8,128,128]{2,1,0:T(8,128)} collective-permute-done((f32[8,128,128]{2,1,0:T(8,128)S(1)}, f32[8,128,128]{2,1,0:T(8,128)}, u32[]{:S(2)}, u32[]{:S(2)}) %collective-permute-start.17) | collective-permute-done | bytes 524320 | tf_op jit(solution)/shard_map/ppermute | solution.py:201
  74.9 3.9 %collective-permute-start.18 = (f32[8,128,128]{2,1,0:T(8,128)}, f32[8,128,128]{2,1,0:T(8,128)}, u32[]{:S(2)}, u32[]{:S(2)}) collective-permute-start(f32[8,128,128]{2,1,0:T(8,128)} %collective-permute-done.17.refs_1_), channel_id=1, source_target_pairs={{2,4},{4,2},{3,5},{5,3},{10,12},{12,10},{11,13},{13,11},{18,20},{2... | collective-permute-start | bytes 1572872 | tf_op jit(solution)/shard_map/ppermute | solution.py:201
  80.3 8.9 %shard_map.28 = (bf16[768,1152]{1,0:T(8,128)(2,1)}, bf16[768,1152]{1,0:T(8,128)(2,1)}, bf16[768,384]{1,0:T(8,128)(2,1)S(1)}, bf16[768,384]{1,0:T(8,128)(2,1)S(1)}) custom-call(s32[5]{0:T(128)S(1)} %pad_add_fusion.place_ref, f32[9,128,256]{2,1,0:T(8,128)S(1)} %copy-done.1, f32[9,128,256]{2,1,0:T(8,128)} %collective-permute-done.15.refs_1_, ...), custom_call_target="tpu_custom_call" | custom-call | flops 1000 | bytes 1000 | tf_op jit(solution)/shard_map/pallas_call | solution.py:65
  89.3 9.0 %shard_map.29 = (f32[2,4,128,128]{3,2,1,0:T(8,128)S(1)}, f32[2,4,128,128]{3,2,1,0:T(8,128)S(1)}, bf16[2,2,2,384,128]{4,3,2,1,0:T(8,128)(2,1)S(1)}) custom-call(s32[4]{0:T(128)S(1)} %iota.18.place_ref, f32[10,128,128]{2,1,0:T(8,128)S(1)} %pad_maximum_fusion.1.refs_0_, f32[10,128,128]{2,1,0:T(8,128)S(1)} %copy-done.8, f32[10,128,128]{2,1,0:T(8,128)S(1)} %copy-done.14, ...), custom_call_target="tpu_custom_call" | custom-call | flops 1000 | bytes 1000 | tf_op jit(solution)/shard_map/pallas_call | solution.py:166
  100.0 11.1 %shard_map.31 = (f32[2,5,128,128]{3,2,1,0:T(8,128)S(1)}, f32[2,5,128,128]{3,2,1,0:T(8,128)S(1)}, bf16[2,2,2,384,128]{4,3,2,1,0:T(8,128)(2,1)S(1)}) custom-call(s32[4]{0:T(128)S(1)} %iota.20.place_ref, f32[10,128,128]{2,1,0:T(8,128)S(1)} %pad_maximum_fusion.refs_0_, f32[10,128,128]{2,1,0:T(8,128)S(1)} %copy-done.16, ...), custom_call_target="tpu_custom_call" | custom-call | flops 1000 | bytes 1000 | tf_op jit(solution)/shard_map/pallas_call | solution.py:166
  111.2 3.9 %collective-permute-start.20 = (f32[8,128,128]{2,1,0:T(8,128)}, f32[8,128,128]{2,1,0:T(8,128)S(1)}, u32[]{:S(2)}, u32[]{:S(2)}) collective-permute-start(f32[8,128,128]{2,1,0:T(8,128)} %collective-permute-done.18.refs_3_), channel_id=1, source_target_pairs={{2,0},{4,6},{3,1},{5,7},{10,8},{12,14},{11,9},{13,15},{18,16},{20,... | collective-permute-start | bytes 1572872 | tf_op jit(solution)/shard_map/ppermute | solution.py:201
  115.2 3.7 %shard_map.30 = (f32[2,4,128,128]{3,2,1,0:T(8,128)S(1)}, f32[2,4,128,128]{3,2,1,0:T(8,128)S(1)}, bf16[2,2,2,128,128]{4,3,2,1,0:T(8,128)(2,1)S(1)}) custom-call(s32[4]{0:T(128)S(1)} %iota.17.place_ref, f32[10,128,128]{2,1,0:T(8,128)S(1)} %copy-done.10, f32[10,128,128]{2,1,0:T(8,128)S(1)} %copy-done.6, f32[2,1,128,128]{3,2,1,0:T(8,128)S(1)} %pad_maximum_fusion.6.refs_2_, ...), custom_call_target="tpu_custom_call" | custom-call | flops 1000 | bytes 1000 | tf_op jit(solution)/shard_map/pallas_call | solution.py:166
  122.4 3.9 %collective-permute-start.25 = (f32[4,128,128]{2,1,0:T(8,128)S(1)}, f32[4,128,128]{2,1,0:T(8,128)S(1)}, u32[]{:S(2)}, u32[]{:S(2)}) collective-permute-start(f32[4,128,128]{2,1,0:T(8,128)S(1)} %collective-permute-done.21.refs_1_), channel_id=1, source_target_pairs={{2,4},{4,2},{3,5},{5,3},{10,12},{12,10},{11,13},{13,11},{18,20},{2... | collective-permute-start | bytes 786440 | tf_op jit(solution)/shard_map/ppermute | solution.py:201
  126.4 5.2 %shard_map.32 = (f32[2,5,128,128]{3,2,1,0:T(8,128)S(1)}, f32[2,5,128,128]{3,2,1,0:T(8,128)S(1)}, bf16[2,2,2,128,128]{4,3,2,1,0:T(8,128)(2,1)S(1)}) custom-call(s32[4]{0:T(128)S(1)} %iota.21.place_ref, f32[10,128,128]{2,1,0:T(8,128)} %collective-permute-done.19.refs_0_, f32[10,128,128]{2,1,0:T(8,128)} %collective-permute-done.13.refs_1_, ...), custom_call_target="tpu_custom_call" | custom-call | flops 1000 | bytes 1000 | tf_op jit(solution)/shard_map/pallas_call | solution.py:166
  133.5 9.3 %shard_map.33 = (f32[2,4,128,128]{3,2,1,0:T(8,128)S(1)}, f32[2,4,128,128]{3,2,1,0:T(8,128)S(1)}, bf16[2,2,2,384,128]{4,3,2,1,0:T(8,128)(2,1)S(1)}) custom-call(s32[4]{0:T(128)S(1)} %iota.22.place_ref, f32[8,128,128]{2,1,0:T(8,128)S(1)} %pad_maximum_fusion.2.refs_0_, f32[8,128,128]{2,1,0:T(8,128)} %collective-permute-done.17.refs_1_, ...), custom_call_target="tpu_custom_call" | custom-call | flops 1000 | bytes 1000 | tf_op jit(solution)/shard_map/pallas_call | solution.py:166
  144.3 4.3 %shard_map.34 = (f32[2,4,128,128]{3,2,1,0:T(8,128)S(1)}, f32[2,4,128,128]{3,2,1,0:T(8,128)S(1)}, bf16[2,2,2,128,128]{4,3,2,1,0:T(8,128)(2,1)S(1)}) custom-call(s32[4]{0:T(128)S(1)} %iota.19.place_ref, f32[8,128,128]{2,1,0:T(8,128)S(1)} %collective-permute-done.20.refs_0_, f32[8,128,128]{2,1,0:T(8,128)} %collective-permute-done.12.refs_1_, ...), custom_call_target="tpu_custom_call" | custom-call | flops 1000 | bytes 1000 | tf_op jit(solution)/shard_map/pallas_call | solution.py:166
  150.4 6.7 %shard_map.35 = (f32[2,3,128,128]{3,2,1,0:T(8,128)S(1)}, f32[2,3,128,128]{3,2,1,0:T(8,128)S(1)}, bf16[2,2,2,384,128]{4,3,2,1,0:T(8,128)(2,1)}) custom-call(s32[4]{0:T(128)S(1)} %iota.24.place_ref, f32[4,128,128]{2,1,0:T(8,128)S(1)} %copy-done.4, f32[4,128,128]{2,1,0:T(8,128)S(1)} %collective-permute-done.21.refs_1_, ...), custom_call_target="tpu_custom_call" | custom-call | flops 1000 | bytes 1000 | tf_op jit(solution)/shard_map/pallas_call | solution.py:166
  157.1 3.6 %shard_map.36 = (f32[2,3,128,128]{3,2,1,0:T(8,128)S(1)}, f32[2,3,128,128]{3,2,1,0:T(8,128)S(1)}, bf16[2,2,2,128,128]{4,3,2,1,0:T(8,128)(2,1)}) custom-call(s32[4]{0:T(128)S(1)} %iota.23.place_ref, f32[4,128,128]{2,1,0:T(8,128)S(1)} %collective-permute-done.26.refs_0_, f32[4,128,128]{2,1,0:T(8,128)S(1)} %collective-permute-done.22.refs_1_, ...), custom_call_target="tpu_custom_call" | custom-call | flops 1000 | bytes 1000 | tf_op jit(solution)/shard_map/pallas_call | solution.py:166
  162.9 8.8 %collective-permute-done.30 = f32[2,3,128,128]{3,2,1,0:T(8,128)S(1)} collective-permute-done((f32[2,3,128,128]{3,2,1,0:T(8,128)S(1)}, f32[2,3,128,128]{3,2,1,0:T(8,128)S(1)}, u32[]{:S(2)}, u32[]{:S(2)}) %collective-permute-start.30) | collective-permute-done | bytes 393248 | tf_op jit(solution)/shard_map/ppermute | solution.py:201
  (118 shorter events, 40.7 us)
Async XLA Ops:
  1.5 17.7 %collective-permute-start.3 = (f32[10,128,128]{2,1,0:T(8,128)S(1)}, f32[10,128,128]{2,1,0:T(8,128)S(1)}, u32[]{:S(2)}, u32[]{:S(2)}) collective-permute-start(f32[10,128,128]{2,1,0:T(8,128)S(1)} %pad_maximum_fusion.1.refs_0_), channel_id=1, source_target_pairs={{0,2},{2,0},{4,6},{6,4},{1,3},{3,1},{5,7},{7,5},{8,10},{10,8},{12,... | collective-permute-start | bytes 1966088 | tf_op jit(solution)/shard_map/ppermute | solution.py:201
  3.2 18.4 %collective-permute-start.1 = (f32[10,128,128]{2,1,0:T(8,128)S(1)}, f32[10,128,128]{2,1,0:T(8,128)S(1)}, u32[]{:S(2)}, u32[]{:S(2)}) collective-permute-start(f32[10,128,128]{2,1,0:T(8,128)S(1)} %pad_maximum_fusion.1.refs_0_), channel_id=1, source_target_pairs={{2,4},{4,2},{3,5},{5,3},{10,12},{12,10},{11,13},{13,11},{18,20},{2... | collective-permute-start | bytes 1966088 | tf_op jit(solution)/shard_map/ppermute | solution.py:201
  5.1 34.0 %collective-permute-start.7 = (f32[9,128,256]{2,1,0:T(8,128)S(1)}, f32[9,128,256]{2,1,0:T(8,128)S(1)}, u32[]{:S(2)}, u32[]{:S(2)}) collective-permute-start(f32[9,128,256]{2,1,0:T(8,128)S(1)} %copy-done.1), channel_id=1, source_target_pairs={{0,8},{8,0},{16,24},{24,16},{1,9},{9,1},{17,25},{25,17},{2,10},{10... | collective-permute-start | bytes 3538952 | tf_op jit(solution)/shard_map/ppermute | solution.py:201
  5.2 27.1 %collective-permute-start = (f32[10,128,128]{2,1,0:T(8,128)S(1)}, f32[10,128,128]{2,1,0:T(8,128)S(1)}, u32[]{:S(2)}, u32[]{:S(2)}) collective-permute-start(f32[10,128,128]{2,1,0:T(8,128)S(1)} %pad_maximum_fusion.refs_0_), channel_id=1, source_target_pairs={{0,2},{2,0},{4,6},{6,4},{1,3},{3,1},{5,7},{7,5},{8,10},{10,8},{12,... | collective-permute-start | bytes 1966088 | tf_op jit(solution)/shard_map/ppermute | solution.py:201
  19.2 16.3 %collective-permute-start.4 = (f32[10,128,128]{2,1,0:T(8,128)S(1)}, f32[10,128,128]{2,1,0:T(8,128)S(1)}, u32[]{:S(2)}, u32[]{:S(2)}) collective-permute-start(f32[10,128,128]{2,1,0:T(8,128)S(1)} %collective-permute-done.3.refs_1_), channel_id=1, source_target_pairs={{2,4},{4,2},{3,5},{5,3},{10,12},{12,10},{11,13},{13,11},{18,20},{2... | collective-permute-start | bytes 1966088 | tf_op jit(solution)/shard_map/ppermute | solution.py:201
  21.6 24.8 %collective-permute-start.6 = (f32[10,128,128]{2,1,0:T(8,128)S(1)}, f32[10,128,128]{2,1,0:T(8,128)S(1)}, u32[]{:S(2)}, u32[]{:S(2)}) collective-permute-start(f32[10,128,128]{2,1,0:T(8,128)S(1)} %collective-permute-done.1.refs_1_), channel_id=1, source_target_pairs={{2,0},{4,6},{3,1},{5,7},{10,8},{12,14},{11,9},{13,15},{18,16},{20,... | collective-permute-start | bytes 1966088 | tf_op jit(solution)/shard_map/ppermute | solution.py:201
  23.5 25.8 %collective-permute-start.15 = (f32[9,128,256]{2,1,0:T(8,128)S(1)}, f32[9,128,256]{2,1,0:T(8,128)}, u32[]{:S(2)}, u32[]{:S(2)}) collective-permute-start(f32[9,128,256]{2,1,0:T(8,128)S(1)} %copy-done.1), channel_id=1, source_target_pairs={{0,16},{8,24},{16,0},{24,8},{1,17},{9,25},{17,1},{25,9},{2,18},{10... | collective-permute-start | bytes 3538952 | tf_op jit(solution)/shard_map/ppermute | solution.py:201
  32.3 19.7 %collective-permute-start.13 = (f32[10,128,128]{2,1,0:T(8,128)S(1)}, f32[10,128,128]{2,1,0:T(8,128)}, u32[]{:S(2)}, u32[]{:S(2)}) collective-permute-start(f32[10,128,128]{2,1,0:T(8,128)S(1)} %pad_maximum_fusion.refs_0_), channel_id=1, source_target_pairs={{2,4},{4,2},{3,5},{5,3},{10,12},{12,10},{11,13},{13,11},{18,20},{2... | collective-permute-start | bytes 1966088 | tf_op jit(solution)/shard_map/ppermute | solution.py:201
  35.5 28.3 %collective-permute-start.2 = (f32[10,128,128]{2,1,0:T(8,128)S(1)}, f32[10,128,128]{2,1,0:T(8,128)}, u32[]{:S(2)}, u32[]{:S(2)}) collective-permute-start(f32[10,128,128]{2,1,0:T(8,128)S(1)} %collective-permute-done.refs_1_), channel_id=1, source_target_pairs={{2,4},{4,2},{3,5},{5,3},{10,12},{12,10},{11,13},{13,11},{18,20},{2... | collective-permute-start | bytes 1966088 | tf_op jit(solution)/shard_map/ppermute | solution.py:201
  39.1 24.8 %collective-permute-start.5 = (f32[10,128,128]{2,1,0:T(8,128)S(1)}, f32[10,128,128]{2,1,0:T(8,128)S(1)}, u32[]{:S(2)}, u32[]{:S(2)}) collective-permute-start(f32[10,128,128]{2,1,0:T(8,128)S(1)} %collective-permute-done.4.refs_3_), channel_id=1, source_target_pairs={{2,0},{4,6},{3,1},{5,7},{10,8},{12,14},{11,9},{13,15},{18,16},{20,... | collective-permute-start | bytes 1966088 | tf_op jit(solution)/shard_map/ppermute | solution.py:201
  49.2 29.8 %collective-permute-start.16 = (f32[9,128,256]{2,1,0:T(8,128)}, f32[9,128,256]{2,1,0:T(8,128)}, u32[]{:S(2)}, u32[]{:S(2)}) collective-permute-start(f32[9,128,256]{2,1,0:T(8,128)} %collective-permute-done.15.refs_1_), channel_id=1, source_target_pairs={{0,8},{8,0},{16,24},{24,16},{1,9},{9,1},{17,25},{25,17},{2,10},{10... | collective-permute-start | bytes 3538952 | tf_op jit(solution)/shard_map/ppermute | solution.py:201
  53.3 18.4 %collective-permute-start.17 = (f32[8,128,128]{2,1,0:T(8,128)S(1)}, f32[8,128,128]{2,1,0:T(8,128)}, u32[]{:S(2)}, u32[]{:S(2)}) collective-permute-start(f32[8,128,128]{2,1,0:T(8,128)S(1)} %pad_maximum_fusion.2.refs_0_), channel_id=1, source_target_pairs={{0,2},{2,0},{4,6},{6,4},{1,3},{3,1},{5,7},{7,5},{8,10},{10,8},{12,... | collective-permute-start | bytes 1572872 | tf_op jit(solution)/shard_map/ppermute | solution.py:201
  54.3 44.0 %collective-permute-start.14 = (f32[10,128,128]{2,1,0:T(8,128)}, f32[10,128,128]{2,1,0:T(8,128)}, u32[]{:S(2)}, u32[]{:S(2)}) collective-permute-start(f32[10,128,128]{2,1,0:T(8,128)} %collective-permute-done.13.refs_1_), channel_id=1, source_target_pairs={{2,0},{4,6},{3,1},{5,7},{10,8},{12,14},{11,9},{13,15},{18,16},{20,... | collective-permute-start | bytes 1966088 | tf_op jit(solution)/shard_map/ppermute | solution.py:201
  63.8 47.3 %collective-permute-start.19 = (f32[10,128,128]{2,1,0:T(8,128)}, f32[10,128,128]{2,1,0:T(8,128)}, u32[]{:S(2)}, u32[]{:S(2)}) collective-permute-start(f32[10,128,128]{2,1,0:T(8,128)} %collective-permute-done.2.refs_3_), channel_id=1, source_target_pairs={{2,0},{4,6},{3,1},{5,7},{10,8},{12,14},{11,9},{13,15},{18,16},{20,... | collective-permute-start | bytes 1966088 | tf_op jit(solution)/shard_map/ppermute | solution.py:201
  73.0 25.4 %collective-permute-start.12 = (f32[8,128,128]{2,1,0:T(8,128)S(1)}, f32[8,128,128]{2,1,0:T(8,128)}, u32[]{:S(2)}, u32[]{:S(2)}) collective-permute-start(f32[8,128,128]{2,1,0:T(8,128)S(1)} %pad_maximum_fusion.2.refs_0_), channel_id=1, source_target_pairs={{2,4},{4,2},{3,5},{5,3},{10,12},{12,10},{11,13},{13,11},{18,20},{2... | collective-permute-start | bytes 1572872 | tf_op jit(solution)/shard_map/ppermute | solution.py:201
  74.9 36.3 %collective-permute-start.18 = (f32[8,128,128]{2,1,0:T(8,128)}, f32[8,128,128]{2,1,0:T(8,128)}, u32[]{:S(2)}, u32[]{:S(2)}) collective-permute-start(f32[8,128,128]{2,1,0:T(8,128)} %collective-permute-done.17.refs_1_), channel_id=1, source_target_pairs={{2,4},{4,2},{3,5},{5,3},{10,12},{12,10},{11,13},{13,11},{18,20},{2... | collective-permute-start | bytes 1572872 | tf_op jit(solution)/shard_map/ppermute | solution.py:201
  98.3 33.8 %collective-permute-start.23 = (f32[8,128,128]{2,1,0:T(8,128)}, f32[8,128,128]{2,1,0:T(8,128)S(1)}, u32[]{:S(2)}, u32[]{:S(2)}) collective-permute-start(f32[8,128,128]{2,1,0:T(8,128)} %collective-permute-done.12.refs_1_), channel_id=1, source_target_pairs={{2,0},{4,6},{3,1},{5,7},{10,8},{12,14},{11,9},{13,15},{18,16},{20,... | collective-permute-start | bytes 1572872 | tf_op jit(solution)/shard_map/ppermute | solution.py:201
  111.2 33.0 %collective-permute-start.20 = (f32[8,128,128]{2,1,0:T(8,128)}, f32[8,128,128]{2,1,0:T(8,128)S(1)}, u32[]{:S(2)}, u32[]{:S(2)}) collective-permute-start(f32[8,128,128]{2,1,0:T(8,128)} %collective-permute-done.18.refs_3_), channel_id=1, source_target_pairs={{2,0},{4,6},{3,1},{5,7},{10,8},{12,14},{11,9},{13,15},{18,16},{20,... | collective-permute-start | bytes 1572872 | tf_op jit(solution)/shard_map/ppermute | solution.py:201
  118.9 29.7 %collective-permute-start.24 = (f32[2,4,128,128]{3,2,1,0:T(8,128)S(1)}, f32[2,4,128,128]{3,2,1,0:T(8,128)S(1)}, u32[]{:S(2)}, u32[]{:S(2)}) collective-permute-start(f32[2,4,128,128]{3,2,1,0:T(8,128)S(1)} %get-tuple-element.119), channel_id=1, source_target_pairs={{0,1},{1,0},{2,3},{3,2},{4,5},{5,4},{6,7},{7,6},{8,9},{9,8},{10,11... | collective-permute-start | bytes 1572872 | tf_op jit(solution)/shard_map/ppermute | solution.py:201
  122.4 20.3 %collective-permute-start.25 = (f32[4,128,128]{2,1,0:T(8,128)S(1)}, f32[4,128,128]{2,1,0:T(8,128)S(1)}, u32[]{:S(2)}, u32[]{:S(2)}) collective-permute-start(f32[4,128,128]{2,1,0:T(8,128)S(1)} %collective-permute-done.21.refs_1_), channel_id=1, source_target_pairs={{2,4},{4,2},{3,5},{5,3},{10,12},{12,10},{11,13},{13,11},{18,20},{2... | collective-permute-start | bytes 786440 | tf_op jit(solution)/shard_map/ppermute | solution.py:201
  131.6 29.1 %collective-permute-start.28 = (f32[2,5,128,128]{3,2,1,0:T(8,128)S(1)}, f32[2,5,128,128]{3,2,1,0:T(8,128)S(1)}, u32[]{:S(2)}, u32[]{:S(2)}) collective-permute-start(f32[2,5,128,128]{3,2,1,0:T(8,128)S(1)} %get-tuple-element.131), channel_id=1, source_target_pairs={{0,1},{1,0},{2,3},{3,2},{4,5},{5,4},{6,7},{7,6},{8,9},{9,8},{10,11... | collective-permute-start | bytes 1966088 | tf_op jit(solution)/shard_map/ppermute | solution.py:201
  132.2 18.2 %collective-permute-start.27 = (f32[4,128,128]{2,1,0:T(8,128)S(1)}, f32[4,128,128]{2,1,0:T(8,128)S(1)}, u32[]{:S(2)}, u32[]{:S(2)}) collective-permute-start(f32[4,128,128]{2,1,0:T(8,128)S(1)} %collective-permute-done.22.refs_1_), channel_id=1, source_target_pairs={{2,0},{4,6},{3,1},{5,7},{10,8},{12,14},{11,9},{13,15},{18,16},{20,... | collective-permute-start | bytes 786440 | tf_op jit(solution)/shard_map/ppermute | solution.py:201
  142.8 14.3 %collective-permute-start.26 = (f32[4,128,128]{2,1,0:T(8,128)S(1)}, f32[4,128,128]{2,1,0:T(8,128)S(1)}, u32[]{:S(2)}, u32[]{:S(2)}) collective-permute-start(f32[4,128,128]{2,1,0:T(8,128)S(1)} %collective-permute-done.25.refs_3_), channel_id=1, source_target_pairs={{2,0},{4,6},{3,1},{5,7},{10,8},{12,14},{11,9},{13,15},{18,16},{20,... | collective-permute-start | bytes 786440 | tf_op jit(solution)/shard_map/ppermute | solution.py:201
  148.7 14.2 %collective-permute-start.29 = (f32[2,4,128,128]{3,2,1,0:T(8,128)S(1)}, f32[2,4,128,128]{3,2,1,0:T(8,128)S(1)}, u32[]{:S(2)}, u32[]{:S(2)}) collective-permute-start(f32[2,4,128,128]{3,2,1,0:T(8,128)S(1)} %get-tuple-element.134), channel_id=1, source_target_pairs={{0,1},{1,0},{2,3},{3,2},{4,5},{5,4},{6,7},{7,6},{8,9},{9,8},{10,11... | collective-permute-start | bytes 1572872 | tf_op jit(solution)/shard_map/ppermute | solution.py:201
  (25 other events, 320.8 us)
